TPU v7x, 128 devices: a whole 4x4x4 slice. The times are simulated.
128 devices in a mesh: ao: 16 (over y, x), aux: 8 (over z, core).
Axes of the slice: x: 4, y: 4, z: 4, core: 2. Of those that a mesh axis runs over, the one named last changes fastest.
Arguments:
- three_centre: bfloat16 [128, 1024, 1024], P('aux', 'ao'), may hold values from -0.26367188 to 0.26367188
- tensor_mask: int32 [16, 16], P('ao'), may hold values 0 or 1
- occ_density: bfloat16 [2, 1024, 1024], P(None, 'ao'), may hold values from -0.1875 to 0.1875
- virt_density: bfloat16 [2, 1024, 1024], P(None, 'ao'), may hold values from -0.1875 to 0.1875
- density_mask: int32 [2, 16, 16], P(None, 'ao'), may hold values 0 or 1
Outputs:
- response: float32 [2, 128, 128], P(None, 'aux', 'ao')
All inputs are finite; a program needn't handle non-finite values. No bound on the sum of `tensor_mask` or of `density_mask` on one device may be relied on, other than what follows from the above.
Results may differ from a plain program's by a relative error of at most 0.0041.
Values may be sent and summed in bfloat16 or wider, within the bound.
No kernel may reach another device: no remote copies, remote signals or barrier semaphores. Data moves between devices by JAX's collectives and lax.ppermute only.
A program may use at most 128 MiB of HBM per device.

v0:
```python
import jax
import jax.numpy as jnp
from jax import lax
from jax.sharding import PartitionSpec as P


def make_contract(occ_now, moved):
    flat = moved[:, 0, :, :]
    paired = jnp.einsum("psm,lm->psl", flat, occ_now, preferred_element_type=jnp.float32)
    return paired.astype(jnp.bfloat16)[:, None, :, :]


def pair_product(left, right):
    left_flat = left.reshape(left.shape[0], -1)
    right_flat = right.reshape(right.shape[0], -1)
    return lax.dot_general(
        left_flat, right_flat, (((1,), (1,)), ((), ())), preferred_element_type=jnp.float32
    )


def body(three_centre, tensor_mask, occ_density, virt_density, density_mask):
    aux_local = three_centre.shape[0]
    block_rows = three_centre.shape[1]
    width_all = three_centre.shape[2]
    blocks_all = width_all // block_rows
    row_mask = jnp.repeat(tensor_mask[0], block_rows).astype(jnp.bfloat16)
    screened = three_centre * row_mask[None, None, :]
    dens_mask = jnp.repeat(density_mask[:, 0, :], block_rows, axis=1).astype(jnp.bfloat16)
    occ_local = occ_density * dens_mask[0][None, None, :]
    virt_local = virt_density * dens_mask[1][None, None, :]
    occ_full, virt_full = (
        lax.all_gather(occ_local, "ao", axis=1, tiled=True),
        lax.all_gather(virt_local, "ao", axis=1, tiled=True),
    )
    screened_view = jnp.transpose(screened, (0, 2, 1)).reshape(
        aux_local, blocks_all, block_rows, block_rows
    )
    halves = []
    for moment in range(2):
        half = jnp.einsum(
            "pmn,ns->psm", screened, virt_full[moment], preferred_element_type=jnp.float32
        )
        halves.append(
            half.astype(jnp.bfloat16).reshape(aux_local, blocks_all, block_rows, block_rows)
        )
    tensor_moved = lax.all_to_all(screened_view, "ao", split_axis=1, concat_axis=3, tiled=True)
    paired_all = []
    for moment in range(2):
        paired_all.append(
            make_contract(
                occ_full[moment],
                lax.all_to_all(halves[moment], "ao", split_axis=1, concat_axis=3, tiled=True),
            )
        )
    piece = lax.all_gather(tensor_moved, "aux", axis=0, tiled=True)
    part = jnp.stack([pair_product(paired_all[moment], piece) for moment in range(2)])
    return lax.psum_scatter(part, "ao", scatter_dimension=2, tiled=True)


def solution(mesh):
    return jax.shard_map(
        body,
        mesh=mesh,
        in_specs=(
            P("aux", "ao", None),
            P("ao", None),
            P(None, "ao", None),
            P(None, "ao", None),
            P(None, "ao", None),
        ),
        out_specs=P(None, "aux", "ao"),
        check_vma=False,
    )
```

profile of v0, /device:TPU:0, one launch (start us, length us, event | category | flops | bytes accessed | tf_op | source)
XLA Modules:
  0.0 353.0 jit_solution(16400536820820362080)
XLA Ops:
  6.5 0.7 convert_element_type.38
  7.2 0.1 broadcast_in_dim.9
  7.3 0.1 mul.28
  7.4 1.7 broadcast_multiply_fusion.1
  9.2 0.1 mul.33
  9.3 1.7 broadcast_multiply_fusion
  11.1 0.7 convert_bitcast_fusion.2
  11.8 0.1 convert_element_type.41
  11.9 1.7 multiply_bitcast_fusion
  13.6 4.0 %reshape.39 = bf16[16,16,64,64]{2,1,3,0:T(8,128)(2,1)} reshape(bf16[16,1024,64]{1,2,0:T(8,128)(2,1)S(1)} %multiply_bitcast_fusion) | data formatting | bytes 4194304 | tf_op jit(solution)/shard_map/reshape | solution.py:35
  17.6 6.8 %copy.23 = bf16[16,16,64,64]{3,2,0,1:T(8,128)(2,1)} copy(bf16[16,16,64,64]{2,1,3,0:T(8,128)(2,1)} %reshape.39) | data formatting | bytes 4194304 | tf_op jit(solution)/shard_map/reshape | solution.py:35
  24.4 6.3 %reshape.49 = bf16[16,2,32768]{2,1,0:T(2,128)(2,1)S(1)} reshape(bf16[16,16,64,64]{3,2,1,0:T(8,128)(2,1)} %bitcast.101) | data formatting | bytes 4194304
  30.8 52.4 %all_to_all.48 = bf16[16,2,32768]{2,1,0:T(2,128)(2,1)} all-to-all(bf16[16,2,32768]{2,1,0:T(2,128)(2,1)S(1)} %reshape.49), channel_id=1, replica_groups=mesh['ao'=16,'aux'=8] {'ao'}, dimensions={0} | all-to-all | bytes 4194304 | tf_op jit(solution)/shard_map/all_to_all | solution.py:46
  83.2 7.4 %reshape.50 = bf16[16,16,64,64]{3,2,1,0:T(8,128)(2,1)} reshape(bf16[16,2,32768]{2,1,0:T(2,128)(2,1)} %all_to_all.48) | data formatting | bytes 4194304
  90.6 3.1 bitcast_bitcast_fusion.1
  93.8 5.5 %copy.24 = bf16[16,1,64,16,64]{4,3,2,0,1:T(8,128)(2,1)} copy(bf16[16,1,64,16,64]{4,2,0,3,1:T(8,128)(2,1)S(1)} %bitcast_bitcast_fusion.1) | data formatting | bytes 4194304 | tf_op jit(solution)/shard_map/all_to_all | solution.py:46
  99.3 6.5 %all_to_all.41 = bf16[16,1,64,1024]{3,2,0,1:T(8,128)(2,1)} reshape(bf16[16,1,64,16,64]{4,3,2,0,1:T(8,128)(2,1)} %copy.24) | data formatting | bytes 4194304 | tf_op jit(solution)/shard_map/all_to_all | solution.py:46
  105.9 4.6 %convert_bitcast_fusion.1 = bf16[16,1024,64]{1,2,0:T(8,128)(2,1)S(1)} fusion(bf16[2,1024,1024]{2,1,0:T(8,128)(2,1)} %all-gather.4.cloned.1.call-done, bf16[16,64,1024]{2,1,0:T(8,128)(2,1)} %param.5, bf16[1024]{0:T(1024)(128)(2,1)S(1)} %convert_element_type.41), kind=kOutput, calls=%fused_computation.9 | convolution fusion | flops 2152726528 | bytes 6293504 | tf_op jit(solution)/shard_map/pmn,ns->psm/dot_general | solution.py:40
  110.4 4.0 %reshape.38 = bf16[16,16,64,64]{2,1,3,0:T(8,128)(2,1)} reshape(bf16[16,1024,64]{1,2,0:T(8,128)(2,1)S(1)} %convert_bitcast_fusion.1) | data formatting | bytes 4194304 | tf_op jit(solution)/shard_map/reshape | solution.py:44
  114.5 5.5 %copy.36 = bf16[16,16,64,64]{2,3,0,1:T(8,128)(2,1)} copy(bf16[16,16,64,64]{2,1,3,0:T(8,128)(2,1)} %reshape.38) | data formatting | bytes 4194304 | tf_op jit(solution)/shard_map/reshape | solution.py:44
  120.0 7.5 %reshape.51 = bf16[16,2,32768]{2,1,0:T(2,128)(2,1)} reshape(bf16[16,16,64,64]{3,2,1,0:T(8,128)(2,1)} %bitcast.102) | data formatting | bytes 4194304
  127.5 4.1 %all-to-all-start = ((bf16[16,2,32768]{2,1,0:T(2,128)(2,1)}), bf16[16,2,32768]{2,1,0:T(2,128)(2,1)S(1)}, u32[]{:S(2)}, u32[]{:S(2)}) async-start(bf16[16,2,32768]{2,1,0:T(2,128)(2,1)} %reshape.51), calls=%async_computation | async-start | bytes 4194304 | tf_op jit(solution)/shard_map/all_to_all | solution.py:52
  131.7 5.9 %convert_bitcast_fusion = bf16[16,1024,64]{1,2,0:T(8,128)(2,1)} fusion(bf16[2,1024,1024]{2,1,0:T(8,128)(2,1)} %all-gather.4.cloned.1.call-done, bf16[16,64,1024]{2,1,0:T(8,128)(2,1)} %param.5, bf16[1024]{0:T(1024)(128)(2,1)S(1)} %convert_element_type.41), kind=kOutput, calls=%fused_computation.8 | convolution fusion | flops 2152726528 | bytes 6293504 | tf_op jit(solution)/shard_map/pmn,ns->psm/dot_general | solution.py:40
  137.6 6.4 %reshape.41 = bf16[16,16,64,64]{2,1,3,0:T(8,128)(2,1)} reshape(bf16[16,1024,64]{1,2,0:T(8,128)(2,1)} %convert_bitcast_fusion) | data formatting | bytes 4194304 | tf_op jit(solution)/shard_map/reshape | solution.py:44
  144.0 5.3 %copy.35 = bf16[16,16,64,64]{2,3,0,1:T(8,128)(2,1)} copy(bf16[16,16,64,64]{2,1,3,0:T(8,128)(2,1)} %reshape.41) | data formatting | bytes 4194304 | tf_op jit(solution)/shard_map/reshape | solution.py:44
  149.3 7.6 %reshape.47 = bf16[16,2,32768]{2,1,0:T(2,128)(2,1)} reshape(bf16[16,16,64,64]{3,2,1,0:T(8,128)(2,1)} %bitcast.103) | data formatting | bytes 4194304
  156.9 5.7 %all-to-all-done = bf16[16,2,32768]{2,1,0:T(2,128)(2,1)S(1)} async-done(((bf16[16,2,32768]{2,1,0:T(2,128)(2,1)}), bf16[16,2,32768]{2,1,0:T(2,128)(2,1)S(1)}, u32[]{:S(2)}, u32[]{:S(2)}) %all-to-all-start) | async-done | bytes 2097184 | tf_op jit(solution)/shard_map/all_to_all | solution.py:52
  162.6 1.3 copy-done
  163.9 3.7 %all-to-all-start.2 = ((bf16[16,2,32768]{2,1,0:T(2,128)(2,1)}), bf16[16,2,32768]{2,1,0:T(2,128)(2,1)S(1)}, u32[]{:S(2)}, u32[]{:S(2)}) async-start(bf16[16,2,32768]{2,1,0:T(2,128)(2,1)} %reshape.47), calls=%async_computation.2 | async-start | bytes 4194304 | tf_op jit(solution)/shard_map/all_to_all | solution.py:52
  167.7 0.6 dynamic-slice
  168.9 7.4 %reshape.52 = bf16[16,16,64,64]{3,2,1,0:T(8,128)(2,1)} reshape(bf16[16,2,32768]{2,1,0:T(2,128)(2,1)} %copy-done) | data formatting | bytes 4194304
  176.4 5.5 %bitcast_bitcast_fusion = bf16[16,1,64,16,64]{2,4,0,3,1:T(8,128)(2,1)} fusion(bf16[16,16,64,64]{3,2,1,0:T(8,128)(2,1)} %reshape.52), kind=kLoop, calls=%fused_computation.26 | loop fusion | bytes 4194304 | tf_op jit(solution)/shard_map/all_to_all | solution.py:52
  181.8 7.1 %copy.22 = bf16[16,1,64,16,64]{4,3,2,0,1:T(8,128)(2,1)} copy(bf16[16,1,64,16,64]{2,4,0,3,1:T(8,128)(2,1)} %bitcast_bitcast_fusion) | data formatting | bytes 4194304 | tf_op jit(solution)/shard_map/all_to_all | solution.py:52
  188.9 6.5 %squeeze.21 = bf16[16,64,1024]{2,1,0:T(8,128)(2,1)} reshape(bf16[16,1,64,16,64]{4,3,2,0,1:T(8,128)(2,1)} %copy.22) | data formatting | bytes 4194304 | tf_op jit(solution)/shard_map/squeeze | solution.py:8
  195.5 4.8 %fusion.4 = bf16[16,64,1024]{2,1,0:T(8,128)(2,1)S(1)} fusion(bf16[16,64,1024]{2,1,0:T(8,128)(2,1)} %squeeze.21, bf16[2,1024,1024]{2,1,0:T(8,128)(2,1)} %all-gather.6.cloned.1.call-done), kind=kOutput, calls=%fused_computation.10 | convolution fusion | flops 2148532224 | bytes 6291456 | tf_op jit(solution)/shard_map/psm,lm->psl/dot_general | solution.py:9
  200.2 2.5 copy.30
  202.8 5.0 %reshape.48 = bf16[16,16,64,64]{3,2,1,0:T(8,128)(2,1)} reshape(bf16[16,2,32768]{2,1,0:T(2,128)(2,1)S(1)} %all-to-all-done.2) | data formatting | bytes 4194304
  207.8 5.6 %bitcast_bitcast_fusion.2 = bf16[16,1,64,16,64]{2,4,0,3,1:T(8,128)(2,1)} fusion(bf16[16,16,64,64]{3,2,1,0:T(8,128)(2,1)} %reshape.48), kind=kLoop, calls=%fused_computation.28 | loop fusion | bytes 4194304 | tf_op jit(solution)/shard_map/all_to_all | solution.py:52
  213.3 7.0 %copy.27 = bf16[16,1,64,16,64]{4,3,2,0,1:T(8,128)(2,1)} copy(bf16[16,1,64,16,64]{2,4,0,3,1:T(8,128)(2,1)} %bitcast_bitcast_fusion.2) | data formatting | bytes 4194304 | tf_op jit(solution)/shard_map/all_to_all | solution.py:52
  220.4 5.6 %squeeze.24 = bf16[16,64,1024]{2,1,0:T(8,128)(2,1)S(1)} reshape(bf16[16,1,64,16,64]{4,3,2,0,1:T(8,128)(2,1)} %copy.27) | data formatting | bytes 4194304 | tf_op jit(solution)/shard_map/squeeze | solution.py:8
  226.0 4.0 %fusion.5 = bf16[16,64,1024]{2,1,0:T(8,128)(2,1)S(1)} fusion(bf16[16,64,1024]{2,1,0:T(8,128)(2,1)S(1)} %squeeze.24, bf16[2,1024,1024]{2,1,0:T(8,128)(2,1)} %all-gather.6.cloned.1.call-done), kind=kOutput, calls=%fused_computation.11 | convolution fusion | flops 2148532224 | bytes 6291456 | tf_op jit(solution)/shard_map/psm,lm->psl/dot_general | solution.py:9
  230.0 2.5 copy.32
  232.4 18.8 %copy.31 = bf16[16,8,64,1024]{3,1,2,0:T(8,128)(2,1)} copy(bf16[16,8,64,1024]{3,2,1,0:T(8,128)(2,1)} %bitcast.100) | data formatting | bytes 33554432
  251.2 8.0 %convolution_bitcast_fusion.1 = f32[1,16,128]{2,1,0:T(8,128)S(1)} fusion(bf16[16,65536]{1,0:T(8,128)(2,1)S(1)} %bitcast.105, bf16[128,65536]{1,0:T(8,128)(2,1)} %bitcast.98), kind=kOutput, calls=%fused_computation.16 | convolution fusion | flops 268435456 | bytes 18882560 | tf_op jit(solution)/shard_map/dot_general | solution.py:16
  259.3 10.8 %convolution_bitcast_fusion = f32[1,16,128]{2,1,0:T(8,128)S(1)} fusion(bf16[16,65536]{1,0:T(8,128)(2,1)} %bitcast.106, bf16[128,65536]{1,0:T(8,128)(2,1)} %bitcast.99), kind=kOutput, calls=%fused_computation.15 | convolution fusion | flops 268435456 | bytes 18882560 | tf_op jit(solution)/shard_map/dot_general | solution.py:16
  270.1 0.1 copy.28
  270.2 75.5 %all-reduce = f32[2,16,128]{1,0,2:T(2,128)S(1)} all-reduce(f32[2,16,128]{1,0,2:T(2,128)S(1)} %copy.28), channel_id=2, replica_groups=mesh['ao'=16,'aux'=8] {'ao'}, use_global_device_ids=true, to_apply=%region_0.0.clone | all-reduce | flops 4096 | bytes 32768
  345.7 0.6 copy.29
  (20 shorter events, 0.3 us)
Async XLA Ops:
  6.5 99.3 %all-gather.4.cloned.1.call-start = ((), (), s32[]{:S(2)}) async-start(), calls=%async_computation.3 | async-start | bytes 4456448 | tf_op jit(solution)/shard_map/all_gather | solution.py:33
  9.1 186.4 %all-gather.6.cloned.1.call-start = ((), (), s32[]{:S(2)}) async-start(), calls=%async_computation.4 | async-start | bytes 4456448 | tf_op jit(solution)/shard_map/all_gather | solution.py:32
  11.0 221.4 %all-gather.8.cloned.1.call-start = ((), (), s32[]{:S(2)}) async-start(), calls=%async_computation.5 | async-start | bytes 18874368 | tf_op jit(solution)/shard_map/all_gather | solution.py:55
  127.5 35.1 %all-to-all-start = ((bf16[16,2,32768]{2,1,0:T(2,128)(2,1)}), bf16[16,2,32768]{2,1,0:T(2,128)(2,1)S(1)}, u32[]{:S(2)}, u32[]{:S(2)}) async-start(bf16[16,2,32768]{2,1,0:T(2,128)(2,1)} %reshape.51), calls=%async_computation | async-start | bytes 4194304 | tf_op jit(solution)/shard_map/all_to_all | solution.py:52
  156.9 10.7 %copy-start.2 = (u32[128]{0:T(128)S(1)}, u32[128]{0:T(128)}, u32[]{:S(2)}) copy-start(u32[128]{0:T(128)} %constant.4) | copy-start | bytes 1540
  162.6 1.3 copy-start
  163.9 38.8 %all-to-all-start.2 = ((bf16[16,2,32768]{2,1,0:T(2,128)(2,1)}), bf16[16,2,32768]{2,1,0:T(2,128)(2,1)S(1)}, u32[]{:S(2)}, u32[]{:S(2)}) async-start(bf16[16,2,32768]{2,1,0:T(2,128)(2,1)} %reshape.47), calls=%async_computation.2 | async-start | bytes 4194304 | tf_op jit(solution)/shard_map/all_to_all | solution.py:52
  232.4 18.8 %copy-start.1 = (bf16[2,8,64,1024]{3,1,2,0:T(8,128)(2,1)S(1)}, bf16[2,8,64,1024]{3,1,2,0:T(8,128)(2,1)}, u32[]{:S(2)}) copy-start(bf16[2,8,64,1024]{3,1,2,0:T(8,128)(2,1)} %copy.30) | copy-start | bytes 6291460
Sparse Core Ops, SparseCore 0:
  9.5 71.6 all-gather.3
  83.4 63.0 all-gather.5
  148.2 82.2 all-gather.7
where the time goes:
time: 358 us; the launch traced here: 353 us
  local copies, waits for them, and re-layouts  153 us (43%)
  blocking collectives  128 us (36%)
  matrix products  38.1 us (11%)
  between operations  14.1 us (4%)
  starting transfers between devices  7.93 us (2%)
  other arithmetic  6.45 us (2%)
  waiting for transfers between devices  5.79 us (2%)
    unnamed x1, blocking collectives  75.5 us
    unnamed x17, local copies, waits for them, and re-layouts  67 us
    all_to_all x1, blocking collectives, body(): lax.all_to_all(screened_view, 'ao', split_axis=1, concat_axis=3, tiled=True)  52.4 us
    all_to_all x4, local copies, waits for them, and re-layouts, body(): lax.all_to_all(halves[moment], 'ao', split_axis=1, concat_axis=3, tiled=T...  25.2 us
    reshape x4, local copies, waits for them, and re-layouts, body(): half.astype(jnp.bfloat16)  21.2 us
    dot_general x2, matrix products, pair_product(): lax.dot_general(left_flat, right_flat, (((1,), (1,)), ((), ())), preferre...  18.9 us
    all_to_all x3, local copies, waits for them, and re-layouts, body(): lax.all_to_all(screened_view, 'ao', split_axis=1, concat_axis=3, tiled=True)  15.2 us
    squeeze x2, local copies, waits for them, and re-layouts, make_contract(): flat = moved[:, 0, :, :]  12.2 us
  transfers between devices with their start and end apart: 5, of which 1 were waited for; matrix products, arithmetic and copies ran while one was open for 42% of the time, Pallas kernels for 0%

commit v1 on v0

v1 whole, which is shorter than its diff:
```python
import jax
import jax.numpy as jnp
from jax import lax
from jax.sharding import PartitionSpec as P

ALL = ("ao", "aux")


def expand(mask_row, width):
    return jnp.repeat(mask_row, width, axis=-1).astype(jnp.bfloat16)


def body(three_centre, tensor_mask, occ_density, virt_density, density_mask):
    per_group, rows, width = three_centre.shape
    blocks = width // rows
    devices = lax.axis_size("ao") * lax.axis_size("aux")
    groups = lax.axis_size("aux")
    slab = width // devices
    moment = lax.axis_index("aux") % 2
    other_core = [(a, a ^ 1) for a in range(groups)]

    screened = three_centre * expand(tensor_mask[0], rows)[None, None, :]
    dens_mask = expand(density_mask[:, 0, :], rows)
    occ_rows = lax.dynamic_index_in_dim(occ_density, moment, 0, False) * dens_mask[0][None, :]
    virt_rows = lax.dynamic_index_in_dim(virt_density, moment, 0, False) * dens_mask[1][None, :]
    dens = lax.all_gather(jnp.stack([virt_rows, occ_rows]), "ao", axis=1, tiled=True)
    virt, occ = dens[0], dens[1]

    own = lax.all_to_all(screened, "ao", split_axis=0, concat_axis=1, tiled=True)[0]
    twin = lax.ppermute(own, "aux", other_core)
    tensor_slab = lax.all_to_all(
        screened.reshape(per_group, groups, slab, width), "aux", split_axis=1, concat_axis=0, tiled=True
    ).reshape(-1, slab, width)

    partials = []
    for matrix in (own, twin):
        half = jnp.dot(matrix, virt, preferred_element_type=jnp.float32).astype(jnp.bfloat16)
        paired = jnp.dot(occ, half, preferred_element_type=jnp.float32).astype(jnp.bfloat16)
        got = lax.all_to_all(
            paired.reshape(devices, slab, width), ALL, split_axis=0, concat_axis=0, tiled=True
        )
        part = lax.dot_general(
            got, tensor_slab, (((1, 2), (1, 2)), ((), ())), preferred_element_type=jnp.float32
        )
        partials.append(part.reshape(blocks, groups // 2, 2, blocks, -1))
    mine, theirs = partials
    first = jnp.stack([mine[:, :, 0], theirs[:, :, 0]], axis=2)
    second = jnp.stack([theirs[:, :, 1], mine[:, :, 1]], axis=2)
    both = jnp.stack([first, second])
    parcels = jnp.transpose(both, (4, 2, 3, 0, 1, 5)).reshape(devices, -1)
    summed = lax.all_to_all(parcels, ALL, split_axis=0, concat_axis=0, tiled=True).sum(axis=0)
    return summed.reshape(2, per_group, -1)


def solution(mesh):
    return jax.shard_map(
        body,
        mesh=mesh,
        in_specs=(
            P("aux", "ao", None),
            P("ao", None),
            P(None, "ao", None),
            P(None, "ao", None),
            P(None, "ao", None),
        ),
        out_specs=P(None, "aux", "ao"),
        check_vma=False,
    )
```

time: 358 us -> 198 us (0.55); the launches traced: 353 us -> 197 us
  local copies, waits for them, and re-layouts: 153 us -> 5.69 us
  blocking collectives: 128 us -> 13.9 us
  waiting for transfers between devices: 5.79 us -> 97.6 us
  starting transfers between devices: 7.93 us -> 28.9 us
  matrix products: 38.1 us -> 30.9 us
    unnamed x1 -> x0, blocking collectives: 75.5 us -> none
    all_to_all x2 -> x4, waiting for transfers between devices: 5.71 us -> 78.5 us  [the longest x2 44.3 us: body(): lax.all_to_all(paired.reshape(devices, slab, width), ALL, split_axis=0, c...]
    unnamed x17 -> x2, local copies, waits for them, and re-layouts: 67 us -> 0.01 us
    all_to_all x7 -> x1, local copies, waits for them, and re-layouts: 40.4 us -> 1.07 us  [body(): lax.all_to_all(parcels, ALL, split_axis=0, concat_axis=0, tiled=True)]
    all_to_all x1, blocking collectives: 52.4 us -> 13.9 us  [body(): lax.all_to_all(parcels, ALL, split_axis=0, concat_axis=0, tiled=True)]
    reshape x6 -> x3, local copies, waits for them, and re-layouts: 32 us -> 2.31 us  [the longest x1 1.55 us: body(): screened.reshape(per_group, groups, slab, width)]
    all_to_all x2 -> x4, starting transfers between devices: 7.84 us -> 28.4 us  [the longest x2 14.9 us: body(): lax.all_to_all(paired.reshape(devices, slab, width), ALL, split_axis=0, c...]
    all_gather x3 -> x1, waiting for transfers between devices: 0.02 us -> 19.1 us  [body(): lax.all_gather(jnp.stack([virt_rows, occ_rows]), 'ao', axis=1, tiled=True)]
  transfers between devices with their start and end apart: 5 -> 6, of which waited for: 1 -> 4; matrix products, arithmetic and copies ran while one was open for 42% -> 15% of each run, Pallas kernels for 0% -> 0%
where the time goes in v1:
time: 198 us; the launch traced here: 197 us
  waiting for transfers between devices  97.6 us (49%)
  matrix products  30.9 us (16%)
  starting transfers between devices  28.9 us (15%)
  blocking collectives  13.9 us (7%)
  between operations  13.5 us (7%)
  other arithmetic  6.64 us (3%)
  local copies, waits for them, and re-layouts  5.69 us (3%)
    all_to_all x2, waiting for transfers between devices, body(): lax.all_to_all(paired.reshape(devices, slab, width), ALL, split_axis=0, c...  44.3 us
    all_to_all x1, waiting for transfers between devices, body(): lax.all_to_all(screened, 'ao', split_axis=0, concat_axis=1, tiled=True)[0]  34.2 us
    all_gather x1, waiting for transfers between devices, body(): lax.all_gather(jnp.stack([virt_rows, occ_rows]), 'ao', axis=1, tiled=True)  19.1 us
    dot_general x2, matrix products, body(): jnp.dot(occ, half, preferred_element_type=jnp.float32).astype(jnp.bfloat16)  17.4 us
    all_to_all x2, starting transfers between devices, body(): lax.all_to_all(paired.reshape(devices, slab, width), ALL, split_axis=0, c...  14.9 us
    all_to_all x1, blocking collectives, body(): lax.all_to_all(parcels, ALL, split_axis=0, concat_axis=0, tiled=True)  13.9 us
    dot_general x2, matrix products, body(): lax.dot_general(got, tensor_slab, (((1, 2), (1, 2)), ((), ())), preferred...  13.5 us
    all_to_all x1, starting transfers between devices, body(): lax.all_to_all(screened, 'ao', split_axis=0, concat_axis=1, tiled=True)[0]  7.3 us
  transfers between devices with their start and end apart: 6, of which 4 were waited for; matrix products, arithmetic and copies ran while one was open for 15% of the time, Pallas kernels for 0%

profile of v1, /device:TPU:0, one launch (start us, length us, event | category | flops | bytes accessed | tf_op | source)
XLA Modules:
  0.0 197.0 jit_solution(1372393846555414867)
XLA Ops:
  6.5 0.0 all-gather.2.cloned.1.call-start
  6.5 0.7 convert_element_type.32
  7.2 0.1 broadcast_in_dim.9
  7.3 0.1 mul.30
  7.4 0.1 broadcast_in_dim.10
  7.5 0.1 mul.33
  7.5 1.0 dynamic-slice_multiply_fusion
  8.5 0.7 pad_maximum_fusion
  9.3 0.0 all-gather.2.cloned.1.call-update
  9.3 0.7 convert_bitcast_fusion.2
  10.0 0.1 broadcast_in_dim.11
  10.1 0.1 convert_element_type.35
  10.1 3.1 %broadcast_multiply_fusion = bf16[16,64,1024]{2,1,0:T(8,128)(2,1)} fusion(bf16[16,64,1024]{2,1,0:T(8,128)(2,1)} %param.5, bf16[1024]{0:T(1024)(128)(2,1)S(1)} %convert_element_type.35), kind=kLoop, calls=%fused_computation.19 | loop fusion | flops 1048576 | bytes 4196352 | tf_op jit(solution)/shard_map/mul | solution.py:22
  13.2 0.0 copy-start
  13.2 7.3 %all-to-all-start = ((bf16[16,64,1024]{2,1,0:T(8,128)(2,1)}), bf16[16,64,1024]{2,1,0:T(8,128)(2,1)}, u32[]{:S(2)}, u32[]{:S(2)}) async-start(bf16[16,64,1024]{2,1,0:T(8,128)(2,1)} %broadcast_multiply_fusion), calls=%async_computation | async-start | bytes 4194304 | tf_op jit(solution)/shard_map/all_to_all | solution.py:29
  20.5 0.0 copy-done
  20.5 0.1 fusion.30
  20.7 1.5 copy.19
  22.2 34.2 %all-to-all-done = bf16[16,64,1024]{2,1,0:T(8,128)(2,1)} async-done(((bf16[16,64,1024]{2,1,0:T(8,128)(2,1)}), bf16[16,64,1024]{2,1,0:T(8,128)(2,1)}, u32[]{:S(2)}, u32[]{:S(2)}) %all-to-all-start) | async-done | bytes 2097184 | tf_op jit(solution)/shard_map/all_to_all | solution.py:29
  56.4 6.2 %all-to-all-start.2 = ((bf16[16,8,8,1024]{3,2,0,1:T(8,128)(2,1)}), bf16[16,8,8,1024]{3,2,0,1:T(8,128)(2,1)S(1)}, u32[]{:S(2)}, u32[]{:S(2)}) async-start(bf16[16,8,8,1024]{3,2,0,1:T(8,128)(2,1)} %copy.19), calls=%async_computation.2 | async-start | bytes 4194304 | tf_op jit(solution)/shard_map/all_to_all | solution.py:31
  62.5 0.5 collective-permute-start
  63.1 19.1 %all-gather.2.cloned.1.call-done = bf16[2,1024,1024]{2,1,0:T(8,128)(2,1)} async-done(((bf16[2,64,1024]{2,1,0:T(8,128)(2,1)}), bf16[2,1024,1024]{2,1,0:T(8,128)(2,1)}) %all-gather.2.cloned.1.call-update) | async-done | bytes 4194320 | tf_op jit(solution)/shard_map/all_gather | solution.py:26
  82.1 8.7 %convert_bitcast_fusion.1 = bf16[128,8,1024]{2,1,0:T(8,128)(2,1)} fusion(bf16[2,1024,1024]{2,1,0:T(8,128)(2,1)} %all-gather.2.cloned.1.call-done, bf16[1024,1024]{1,0:T(8,128)(2,1)} %bitcast.4), kind=kOutput, calls=%fused_computation.9 | convolution fusion | flops 4297064448 | bytes 8388608 | tf_op jit(solution)/shard_map/dot_general | solution.py:38
  90.8 0.0 all-to-all-done.2
  90.8 8.9 %all-to-all-start.1 = ((bf16[128,8,1024]{2,1,0:T(8,128)(2,1)}), bf16[128,8,1024]{2,1,0:T(8,128)(2,1)}, u32[]{:S(2)}, u32[]{:S(2)}) async-start(bf16[128,8,1024]{2,1,0:T(8,128)(2,1)} %convert_bitcast_fusion.1), calls=%async_computation.1 | async-start | bytes 4194304 | tf_op jit(solution)/shard_map/all_to_all | solution.py:39
  99.8 0.0 collective-permute-done
  99.8 8.7 %convert_bitcast_fusion = bf16[128,8,1024]{2,1,0:T(8,128)(2,1)} fusion(bf16[2,1024,1024]{2,1,0:T(8,128)(2,1)} %all-gather.2.cloned.1.call-done, bf16[1024,1024]{1,0:T(8,128)(2,1)} %collective-permute-done), kind=kOutput, calls=%fused_computation.6 | convolution fusion | flops 4297064448 | bytes 8388608 | tf_op jit(solution)/shard_map/dot_general | solution.py:38
  108.5 21.3 %all-to-all-done.1 = bf16[128,8,1024]{2,1,0:T(8,128)(2,1)} async-done(((bf16[128,8,1024]{2,1,0:T(8,128)(2,1)}), bf16[128,8,1024]{2,1,0:T(8,128)(2,1)}, u32[]{:S(2)}, u32[]{:S(2)}) %all-to-all-start.1) | async-done | bytes 2097184 | tf_op jit(solution)/shard_map/all_to_all | solution.py:39
  129.8 6.0 %all-to-all-start.3 = ((bf16[128,8,1024]{2,1,0:T(8,128)(2,1)}), bf16[128,8,1024]{2,1,0:T(8,128)(2,1)}, u32[]{:S(2)}, u32[]{:S(2)}) async-start(bf16[128,8,1024]{2,1,0:T(8,128)(2,1)} %convert_bitcast_fusion), calls=%async_computation.3 | async-start | bytes 4194304 | tf_op jit(solution)/shard_map/all_to_all | solution.py:39
  135.7 6.8 %fusion.16 = f32[16,4,2,16,8]{3,0,4,2,1:T(8,128)S(1)} fusion(bf16[16,8,8,1024,1,1]{3,2,1,0,5,4:T(8,128)(2,1)S(1)} %bitcast.59, bf16[16,4,2,8,1024,1]{4,3,2,1,0,5:T(8,128)(2,1)} %bitcast.8), kind=kOutput, calls=%fused_computation.16 | convolution fusion | flops 268435456 | bytes 4259840 | tf_op jit(solution)/shard_map/dot_general | solution.py:42
  142.6 23.0 %all-to-all-done.3 = bf16[128,8,1024]{2,1,0:T(8,128)(2,1)} async-done(((bf16[128,8,1024]{2,1,0:T(8,128)(2,1)}), bf16[128,8,1024]{2,1,0:T(8,128)(2,1)}, u32[]{:S(2)}, u32[]{:S(2)}) %all-to-all-start.3) | async-done | bytes 2097184 | tf_op jit(solution)/shard_map/all_to_all | solution.py:39
  165.6 6.8 %fusion.21 = f32[16,4,2,16,8]{3,0,4,2,1:T(8,128)S(1)} fusion(bf16[16,8,8,1024,1,1]{3,2,1,0,5,4:T(8,128)(2,1)S(1)} %bitcast.60, bf16[16,4,2,8,1024,1]{4,3,2,1,0,5:T(8,128)(2,1)} %bitcast.18), kind=kOutput, calls=%fused_computation.17 | convolution fusion | flops 268435456 | bytes 4259840 | tf_op jit(solution)/shard_map/dot_general | solution.py:42
  172.5 0.1 maximum_bitcast_fusion
  172.6 1.7 copy.24
  174.3 1.1 all_to_all.38
  175.4 13.9 %all_to_all.44 = f32[128,1,256]{2,1,0:T(1,128)S(1)} all-to-all(f32[128,1,256]{2,1,0:T(1,128)S(1)} %all_to_all.38), channel_id=1, replica_groups=mesh['ao'=16,'aux'=8] {'ao','aux'}, dimensions={0} | all-to-all | bytes 262144 | tf_op jit(solution)/shard_map/all_to_all | solution.py:51
  189.3 0.2 reduce_sum.9
  189.4 0.1 reshape.66
  189.5 0.7 copy.26
  (5 shorter events, 0.2 us)
Async XLA Ops:
  6.5 75.6 %all-gather.2.cloned.1.call-start = ((), (), s32[]{:S(2)}) async-start(), calls=%async_computation.5 | async-start | bytes 4456448 | tf_op jit(solution)/shard_map/all_gather | solution.py:26
  13.2 7.3 %copy-start = (bf16[16,64,1024]{2,1,0:T(8,128)(2,1)S(1)}, bf16[16,64,1024]{2,1,0:T(8,128)(2,1)}, u32[]{:S(2)}) copy-start(bf16[16,64,1024]{2,1,0:T(8,128)(2,1)} %param.5) | copy-start | bytes 6291460
  13.2 43.2 %all-to-all-start = ((bf16[16,64,1024]{2,1,0:T(8,128)(2,1)}), bf16[16,64,1024]{2,1,0:T(8,128)(2,1)}, u32[]{:S(2)}, u32[]{:S(2)}) async-start(bf16[16,64,1024]{2,1,0:T(8,128)(2,1)} %broadcast_multiply_fusion), calls=%async_computation | async-start | bytes 4194304 | tf_op jit(solution)/shard_map/all_to_all | solution.py:29
  56.4 34.4 %all-to-all-start.2 = ((bf16[16,8,8,1024]{3,2,0,1:T(8,128)(2,1)}), bf16[16,8,8,1024]{3,2,0,1:T(8,128)(2,1)S(1)}, u32[]{:S(2)}, u32[]{:S(2)}) async-start(bf16[16,8,8,1024]{3,2,0,1:T(8,128)(2,1)} %copy.19), calls=%async_computation.2 | async-start | bytes 4194304 | tf_op jit(solution)/shard_map/all_to_all | solution.py:31
  62.5 37.2 %collective-permute-start = (bf16[1024,1024]{1,0:T(8,128)(2,1)}, bf16[1024,1024]{1,0:T(8,128)(2,1)}, u32[]{:S(2)}, u32[]{:S(2)}) collective-permute-start(bf16[1024,1024]{1,0:T(8,128)(2,1)} %bitcast.4), channel_id=1, source_target_pairs={{0,1},{1,0},{2,3},{3,2},{4,5},{5,4},{6,7},{7,6},{8,9},{9,8},{10,11... | collective-permute-start | bytes 6291464 | tf_op jit(solution)/shard_map/ppermute | solution.py:30
  90.8 38.9 %all-to-all-start.1 = ((bf16[128,8,1024]{2,1,0:T(8,128)(2,1)}), bf16[128,8,1024]{2,1,0:T(8,128)(2,1)}, u32[]{:S(2)}, u32[]{:S(2)}) async-start(bf16[128,8,1024]{2,1,0:T(8,128)(2,1)} %convert_bitcast_fusion.1), calls=%async_computation.1 | async-start | bytes 4194304 | tf_op jit(solution)/shard_map/all_to_all | solution.py:39
  129.8 35.8 %all-to-all-start.3 = ((bf16[128,8,1024]{2,1,0:T(8,128)(2,1)}), bf16[128,8,1024]{2,1,0:T(8,128)(2,1)}, u32[]{:S(2)}, u32[]{:S(2)}) async-start(bf16[128,8,1024]{2,1,0:T(8,128)(2,1)} %convert_bitcast_fusion), calls=%async_computation.3 | async-start | bytes 4194304 | tf_op jit(solution)/shard_map/all_to_all | solution.py:39
Sparse Core Ops, SparseCore 0:
  9.5 72.5 all-gather.1

commit v2 on v1

v2 whole, which is shorter than its diff:
```python
import jax
import jax.numpy as jnp
from jax import lax
from jax.sharding import PartitionSpec as P

ALL = ("ao", "aux")
SIDE = 4
CORES = 2


def expand(mask_row, width):
    return jnp.repeat(mask_row, width, axis=-1).astype(jnp.bfloat16)


def along_x(step):
    return [(i, (i // SIDE) * SIDE + (i % SIDE + step) % SIDE) for i in range(SIDE * SIDE)]


def along_y(step):
    return [(i, ((i // SIDE + step) % SIDE) * SIDE + i % SIDE) for i in range(SIDE * SIDE)]


def along_z(step):
    return [(k, ((k // CORES + step) % SIDE) * CORES + k % CORES) for k in range(SIDE * CORES)]


OTHER_CORE = [(k, k ^ 1) for k in range(SIDE * CORES)]
SAME_CORE = [
    [i * SIDE * CORES + CORES * z + core for i in range(SIDE * SIDE) for z in range(SIDE)]
    for core in range(CORES)
]
OFFSETS = (0, -1, 1, 2)


def ring(rows, step):
    before = lax.ppermute(rows, "ao", step(1))
    after = lax.ppermute(rows, "ao", step(-1))
    far = lax.ppermute(after, "ao", step(-1))
    return rows, before, after, far


def place(pieces, spot):
    whole = jnp.zeros((SIDE,) + pieces[0].shape, pieces[0].dtype)
    for offset, piece in zip(OFFSETS, pieces):
        whole = lax.dynamic_update_index_in_dim(whole, piece, (spot + offset) % SIDE, 0)
    return whole


def body(three_centre, tensor_mask, occ_density, virt_density, density_mask):
    per_group, rows, width = three_centre.shape
    chips = SIDE**3
    slab = width // chips
    spot = lax.axis_index("ao")
    x, y = spot % SIDE, spot // SIDE
    z, core = lax.axis_index("aux") // CORES, lax.axis_index("aux") % CORES

    dens_mask = expand(density_mask[:, 0, :], rows)
    virt_rows = lax.dynamic_index_in_dim(virt_density, core, 0, False) * dens_mask[1][None, :]
    occ_rows = lax.dynamic_index_in_dim(occ_density, core, 0, False) * dens_mask[0][None, :]
    virt_near = ring(virt_rows, along_x)
    occ_near = ring(occ_rows, along_y)
    virt_row = jnp.concatenate(virt_near, 0)
    occ_row = jnp.concatenate(occ_near, 0)
    virt_far = ring(virt_row, along_y)
    occ_far = ring(occ_row, along_x)
    virt = place([place(list(v.reshape(SIDE, rows, width)), x) for v in virt_far], y)
    occ = place([place(list(o.reshape(SIDE, rows, width)), y) for o in occ_far], x)
    virt = virt.reshape(width, width)
    occ = jnp.swapaxes(occ, 0, 1).reshape(width, width)

    screened = three_centre * expand(tensor_mask[0], rows)[None, None, :]
    own = lax.all_to_all(screened, "ao", split_axis=0, concat_axis=1, tiled=True)[0]
    twin = lax.ppermute(own, "aux", OTHER_CORE)

    def cut(offset):
        view = screened.reshape(per_group, SIDE, slab, width)
        return lax.dynamic_index_in_dim(view, (z + offset) % SIDE, 1, False)

    far, cut_at = cut(2), per_group // 2
    before = lax.ppermute(jnp.concatenate([cut(1), far[:cut_at]]), "aux", along_z(1))
    after = lax.ppermute(jnp.concatenate([cut(-1), far[cut_at:]]), "aux", along_z(-1))
    opposite = jnp.concatenate(
        [
            lax.ppermute(before[per_group:], "aux", along_z(1)),
            lax.ppermute(after[per_group:], "aux", along_z(-1)),
        ]
    )
    slabs = place([cut(0), before[:per_group], after[:per_group], opposite], z)
    slabs_twin = lax.ppermute(slabs, "aux", OTHER_CORE)
    tensor_slab = jnp.where(
        core == 0, jnp.stack([slabs, slabs_twin], 1), jnp.stack([slabs_twin, slabs], 1)
    ).reshape(-1, slab, width)

    products = []
    for matrix in (own, twin):
        half = jnp.dot(matrix, virt, preferred_element_type=jnp.float32).astype(jnp.bfloat16)
        paired = jnp.dot(occ, half, preferred_element_type=jnp.float32).astype(jnp.bfloat16)
        products.append(paired.reshape(chips, slab, width))
    got = lax.all_to_all(
        jnp.stack(products, 1), ALL, split_axis=0, concat_axis=0, tiled=True, axis_index_groups=SAME_CORE
    )
    part = lax.dot_general(
        got, tensor_slab, (((2, 3), (1, 2)), ((), ())), preferred_element_type=jnp.float32
    )
    part = part.reshape(SIDE * SIDE, SIDE, CORES, SIDE * SIDE, -1)
    parcels = jnp.transpose(part, (3, 1, 2, 0, 4)).reshape(chips, -1)
    summed = lax.all_to_all(
        parcels, ALL, split_axis=0, concat_axis=0, tiled=True, axis_index_groups=SAME_CORE
    ).sum(axis=0).reshape(CORES, per_group, -1)
    mine, theirs = summed[0], lax.ppermute(summed[1], "aux", OTHER_CORE)
    return jnp.where(core == 0, jnp.stack([mine, theirs]), jnp.stack([theirs, mine]))


def solution(mesh):
    return jax.shard_map(
        body,
        mesh=mesh,
        in_specs=(
            P("aux", "ao", None),
            P("ao", None),
            P(None, "ao", None),
            P(None, "ao", None),
            P(None, "ao", None),
        ),
        out_specs=P(None, "aux", "ao"),
        check_vma=False,
    )
```

time: 198 us -> 244 us (1.23)
  local copies, waits for them, and re-layouts: 5.69 us -> 35.1 us
  starting transfers between devices: 28.9 us -> 49.3 us
  between operations: 13.5 us -> 0.75 us
  other arithmetic: 6.64 us -> 17.3 us
  waiting for transfers between devices: 97.6 us -> 89.8 us
  blocking collectives: 13.9 us -> 18.4 us
    ppermute x1 -> x19, waiting for transfers between devices: 0.01 us -> 89.8 us  [the longest x1 58.8 us: body(): lax.ppermute(jnp.concatenate([cut(-1), far[cut_at:]]), 'aux', along_z(-1))]
    all_to_all x3 -> x1, waiting for transfers between devices: 44.3 us -> 0.01 us  [body(): lax.all_to_all(jnp.stack(products, 1), ALL, split_axis=0, concat_axis=0,...]
    all_to_all x1, waiting for transfers between devices: 34.2 us -> 0.01 us  [body(): lax.all_to_all(screened, 'ao', split_axis=0, concat_axis=1, tiled=True)[0]]
    ppermute x1 -> x19, starting transfers between devices: 0.51 us -> 28.4 us  [the longest x4 10.3 us: ring(): after = lax.ppermute(rows, 'ao', step(-1))]
    dynamic_update_slice x0 -> x42, local copies, waits for them, and re-layouts: none -> 22.9 us  [place(): lax.dynamic_update_index_in_dim(whole, piece, (spot + offset) % SIDE, 0)]
    all_gather x1 -> x0, waiting for transfers between devices: 19.1 us -> none  [body(): lax.all_gather(jnp.stack([virt_rows, occ_rows]), 'ao', axis=1, tiled=True)]
    all_to_all x3 -> x1, starting transfers between devices: 21.1 us -> 13.4 us  [body(): lax.all_to_all(jnp.stack(products, 1), ALL, split_axis=0, concat_axis=0,...]
    all_to_all x1, blocking collectives: 13.9 us -> 18.4 us  [body(): lax.all_to_all(parcels, ALL, split_axis=0, concat_axis=0, tiled=True, axi...]
  transfers between devices with their start and end apart: 6 -> 21, of which waited for: 4 -> 8; matrix products, arithmetic and copies ran while one was open for 15% -> 21% of each run, Pallas kernels for 0% -> 0%
where the time goes in v2:
time: 244 us; the launch traced here: 242 us
  waiting for transfers between devices  89.8 us (37%)
  starting transfers between devices  49.3 us (20%)
  local copies, waits for them, and re-layouts  35.1 us (14%)
  matrix products  31.6 us (13%)
  blocking collectives  18.4 us (8%)
  other arithmetic  17.3 us (7%)
    ppermute x1, waiting for transfers between devices, body(): lax.ppermute(jnp.concatenate([cut(-1), far[cut_at:]]), 'aux', along_z(-1))  58.8 us
    dynamic_update_slice x42, local copies, waits for them, and re-layouts, place(): lax.dynamic_update_index_in_dim(whole, piece, (spot + offset) % SIDE, 0)  22.9 us
    all_to_all x1, blocking collectives, body(): lax.all_to_all(parcels, ALL, split_axis=0, concat_axis=0, tiled=True, axi...  18.4 us
    dot_general x2, matrix products, body(): jnp.dot(occ, half, preferred_element_type=jnp.float32).astype(jnp.bfloat16)  16.2 us
    ppermute x4, waiting for transfers between devices, ring(): far = lax.ppermute(after, 'ao', step(-1))  16.1 us
    dot_general x1, matrix products, body(): lax.dot_general(got, tensor_slab, (((2, 3), (1, 2)), ((), ())), preferred...  15.4 us
    all_to_all x1, starting transfers between devices, body(): lax.all_to_all(jnp.stack(products, 1), ALL, split_axis=0, concat_axis=0,...  13.4 us
    ppermute x4, starting transfers between devices, ring(): after = lax.ppermute(rows, 'ao', step(-1))  10.3 us
  transfers between devices with their start and end apart: 21, of which 8 were waited for; matrix products, arithmetic and copies ran while one was open for 21% of the time, Pallas kernels for 0%

profile of v2, /device:TPU:0, one launch (start us, length us, event | category | flops | bytes accessed | tf_op | source)
XLA Modules:
  0.0 242.2 jit_solution(4910841814990138660)
XLA Ops:
  1.8 2.9 %collective-permute-start.7 = (bf16[64,1024]{1,0:T(8,128)(2,1)S(1)}, bf16[64,1024]{1,0:T(8,128)(2,1)S(1)}, u32[]{:S(2)}, u32[]{:S(2)}) collective-permute-start(bf16[64,1024]{1,0:T(8,128)(2,1)S(1)} %bitcast_multiply_fusion), channel_id=1, source_target_pairs={{0,24},{8,0},{16,8},{24,16},{32,56},{40,32},{48,40},{56,48},{64,88... | collective-permute-start | bytes 393224 | tf_op jit(solution)/shard_map/ppermute | solution.py:37
  5.8 3.1 %collective-permute-start.1 = (bf16[64,1024]{1,0:T(8,128)(2,1)S(1)}, bf16[64,1024]{1,0:T(8,128)(2,1)S(1)}, u32[]{:S(2)}, u32[]{:S(2)}) collective-permute-start(bf16[64,1024]{1,0:T(8,128)(2,1)S(1)} %bitcast_multiply_fusion.2), channel_id=1, source_target_pairs={{0,96},{8,104},{16,112},{24,120},{32,0},{40,8},{48,16},{56,24},{64... | collective-permute-start | bytes 393224 | tf_op jit(solution)/shard_map/ppermute | solution.py:37
  9.7 3.1 %broadcast_multiply_fusion = bf16[16,64,1024]{2,1,0:T(8,128)(2,1)} fusion(bf16[16,64,1024]{2,1,0:T(8,128)(2,1)} %param.5, bf16[1024]{0:T(1024)(128)(2,1)S(1)} %convert_element_type.35), kind=kLoop, calls=%fused_computation.14 | loop fusion | flops 1048576 | bytes 4196352 | tf_op jit(solution)/shard_map/mul | solution.py:71
  12.8 7.5 %all-to-all-start = ((bf16[16,64,1024]{2,1,0:T(8,128)(2,1)}), bf16[16,64,1024]{2,1,0:T(8,128)(2,1)}, u32[]{:S(2)}, u32[]{:S(2)}) async-start(bf16[16,64,1024]{2,1,0:T(8,128)(2,1)} %broadcast_multiply_fusion), calls=%async_computation | async-start | bytes 4194304 | tf_op jit(solution)/shard_map/all_to_all | solution.py:72
  22.0 1.3 dynamic-slice_bitcast_fusion
  23.5 1.8 dynamic-slice_bitcast_fusion.2
  25.3 3.0 %collective-permute-start.8 = (bf16[64,1024]{1,0:T(8,128)(2,1)S(1)}, bf16[64,1024]{1,0:T(8,128)(2,1)S(1)}, u32[]{:S(2)}, u32[]{:S(2)}) collective-permute-start(bf16[64,1024]{1,0:T(8,128)(2,1)S(1)} %collective-permute-done.7), channel_id=1, source_target_pairs={{0,24},{8,0},{16,8},{24,16},{32,56},{40,32},{48,40},{56,48},{64,88... | collective-permute-start | bytes 393224 | tf_op jit(solution)/shard_map/ppermute | solution.py:38
  28.3 2.7 %collective-permute-start.2 = (bf16[64,1024]{1,0:T(8,128)(2,1)S(1)}, bf16[64,1024]{1,0:T(8,128)(2,1)S(1)}, u32[]{:S(2)}, u32[]{:S(2)}) collective-permute-start(bf16[64,1024]{1,0:T(8,128)(2,1)S(1)} %collective-permute-done.1), channel_id=1, source_target_pairs={{0,96},{8,104},{16,112},{24,120},{32,0},{40,8},{48,16},{56,24},{64... | collective-permute-start | bytes 393224 | tf_op jit(solution)/shard_map/ppermute | solution.py:38
  32.4 16.1 %collective-permute-done.8 = bf16[64,1024]{1,0:T(8,128)(2,1)S(1)} collective-permute-done((bf16[64,1024]{1,0:T(8,128)(2,1)S(1)}, bf16[64,1024]{1,0:T(8,128)(2,1)S(1)}, u32[]{:S(2)}, u32[]{:S(2)}) %collective-permute-start.8) | collective-permute-done | bytes 131104 | tf_op jit(solution)/shard_map/ppermute | solution.py:38
  49.3 2.6 %collective-permute-start.10 = (bf16[256,1024]{1,0:T(8,128)(2,1)S(1)}, bf16[256,1024]{1,0:T(8,128)(2,1)S(1)}, u32[]{:S(2)}, u32[]{:S(2)}) collective-permute-start(bf16[256,1024]{1,0:T(8,128)(2,1)S(1)} %pad_maximum_fusion.4), channel_id=1, source_target_pairs={{0,96},{8,104},{16,112},{24,120},{32,0},{40,8},{48,16},{56,24},{64... | collective-permute-start | bytes 1572872 | tf_op jit(solution)/shard_map/ppermute | solution.py:37
  51.9 1.6 collective-permute-start.3
  53.5 1.7 collective-permute-start.4
  56.1 1.1 constant_dynamic-update-slice_fusion.3
  57.3 1.6 broadcast.72.clone
  59.7 1.5 collective-permute-done.9
  61.4 2.8 %collective-permute-start.11 = (bf16[256,1024]{1,0:T(8,128)(2,1)S(1)}, bf16[256,1024]{1,0:T(8,128)(2,1)S(1)}, u32[]{:S(2)}, u32[]{:S(2)}) collective-permute-start(bf16[256,1024]{1,0:T(8,128)(2,1)S(1)} %collective-permute-done.10), channel_id=1, source_target_pairs={{0,96},{8,104},{16,112},{24,120},{32,0},{40,8},{48,16},{56,24},{64... | collective-permute-start | bytes 1572872 | tf_op jit(solution)/shard_map/ppermute | solution.py:38
  64.6 1.4 collective-permute-done.4
  66.0 1.5 collective-permute-start.5
  67.5 0.9 fusion.44
  68.5 0.9 fusion.43
  69.5 0.9 fusion.42
  76.6 1.1 constant_dynamic-update-slice_fusion
  77.7 1.6 copy.113
  79.3 1.1 fusion.40
  80.4 0.9 fusion.39
  81.3 0.9 fusion.38
  82.3 0.9 fusion.37
  84.0 8.1 %fusion.7 = bf16[1024,1024]{1,0:T(8,128)(2,1)} fusion(bf16[1024,1024]{1,0:T(8,128)(2,1)} %bitcast.33, bf16[1024,1024]{1,0:T(8,128)(2,1)} %bitcast.35, bf16[1024,1024]{1,0:T(8,128)(2,1)S(1)} %bitcast.240), kind=kOutput, calls=%fused_computation.9 | convolution fusion | flops 4297064448 | bytes 8388608 | tf_op jit(solution)/shard_map/dot_general | solution.py:97
  92.1 8.1 %fusion.10 = bf16[1024,1024]{1,0:T(8,128)(2,1)} fusion(bf16[1024,1024]{1,0:T(8,128)(2,1)} %bitcast.33, bf16[1024,1024]{1,0:T(8,128)(2,1)} %collective-permute-done.12, bf16[1024,1024]{1,0:T(8,128)(2,1)S(1)} %bitcast.241), kind=kOutput, calls=%fused_computation.10 | convolution fusion | flops 4297064448 | bytes 8388608 | tf_op jit(solution)/shard_map/dot_general | solution.py:97
  100.2 4.6 %pad_maximum_fusion = bf16[64,2,16,1024]{3,2,1,0:T(8,128)(2,1)} fusion(bf16[64,1,16,1024]{3,2,1,0:T(8,128)(2,1)} %bitcast.243, bf16[64,1,16,1024]{3,2,1,0:T(8,128)(2,1)} %bitcast.242), kind=kLoop, calls=%fused_computation | loop fusion | flops 2097152 | bytes 8388608 | tf_op jit(solution)/shard_map/stack | solution.py:100
  104.8 13.4 %all-to-all-start.1 = ((bf16[64,2,16,1024]{3,2,1,0:T(8,128)(2,1)}), bf16[64,2,16,1024]{3,2,1,0:T(8,128)(2,1)}, u32[]{:S(2)}, u32[]{:S(2)}) async-start(bf16[64,2,16,1024]{3,2,1,0:T(8,128)(2,1)} %pad_maximum_fusion), calls=%async_computation.1 | async-start | bytes 8388608 | tf_op jit(solution)/shard_map/all_to_all | solution.py:99
  118.3 2.8 %collective-permute-start.14 = (bf16[24,16,1024]{2,1,0:T(8,128)(2,1)S(1)}, bf16[24,16,1024]{2,1,0:T(8,128)(2,1)}, u32[]{:S(2)}, u32[]{:S(2)}) collective-permute-start(bf16[24,16,1024]{2,1,0:T(8,128)(2,1)S(1)} %pad_maximum_fusion.2), channel_id=1, source_target_pairs={{0,6},{1,7},{2,0},{3,1},{4,2},{5,3},{6,4},{7,5},{8,14},{9,15},{10,... | collective-permute-start | bytes 2359304 | tf_op jit(solution)/shard_map/ppermute | solution.py:81
  121.1 1.0 pad_maximum_fusion.1
  122.3 1.1 bitcast_dynamic-update-slice_fusion
  123.4 58.8 %collective-permute-done.14 = bf16[24,16,1024]{2,1,0:T(8,128)(2,1)} collective-permute-done((bf16[24,16,1024]{2,1,0:T(8,128)(2,1)S(1)}, bf16[24,16,1024]{2,1,0:T(8,128)(2,1)}, u32[]{:S(2)}, u32[]{:S(2)}) %collective-permute-start.14) | collective-permute-done | bytes 786464 | tf_op jit(solution)/shard_map/ppermute | solution.py:81
  182.2 1.0 slice.118
  183.1 2.6 %collective-permute-start.16 = (bf16[8,16,1024]{2,1,0:T(8,128)(2,1)S(1)}, bf16[8,16,1024]{2,1,0:T(8,128)(2,1)S(1)}, u32[]{:S(2)}, u32[]{:S(2)}) collective-permute-start(bf16[8,16,1024]{2,1,0:T(8,128)(2,1)S(1)} %slice.118), channel_id=1, source_target_pairs={{0,6},{1,7},{2,0},{3,1},{4,2},{5,3},{6,4},{7,5},{8,14},{9,15},{10,... | collective-permute-start | bytes 786440 | tf_op jit(solution)/shard_map/ppermute | solution.py:85
  185.8 1.0 slice.117
  186.8 1.1 fusion.23
  187.9 1.1 fusion.22
  189.0 2.1 collective-permute-done.16
  191.1 4.5 %collective-permute-done.15 = bf16[8,16,1024]{2,1,0:T(8,128)(2,1)S(1)} collective-permute-done((bf16[8,16,1024]{2,1,0:T(8,128)(2,1)S(1)}, bf16[8,16,1024]{2,1,0:T(8,128)(2,1)S(1)}, u32[]{:S(2)}, u32[]{:S(2)}) %collective-permute-start.15) | collective-permute-done | bytes 262176 | tf_op jit(solution)/shard_map/ppermute | solution.py:84
  195.9 4.3 %collective-permute-done.17 = bf16[4,16,16,1024]{3,2,1,0:T(8,128)(2,1)} collective-permute-done((bf16[4,16,16,1024]{3,2,1,0:T(8,128)(2,1)S(1)}, bf16[4,16,16,1024]{3,2,1,0:T(8,128)(2,1)}, u32[]{:S(2)}, u32[]{:S(2)}) %collective-permute-start.17) | collective-permute-done | bytes 2097184 | tf_op jit(solution)/shard_map/ppermute | solution.py:89
  200.2 4.5 %maximum_select_fusion = bf16[4,2,16,16,1024]{4,3,2,1,0:T(8,128)(2,1)} fusion(bf16[4,1,16,16,1024]{4,3,2,1,0:T(8,128)(2,1)} %bitcast.86, bf16[4,1,16,16,1024]{4,3,2,1,0:T(8,128)(2,1)S(1)} %bitcast.238, pred[]{:T(512)S(6)} %eq.55), kind=kLoop, calls=%fused_computation.1 | loop fusion | flops 6291456 | bytes 8388609 | tf_op jit(solution)/shard_map/jit(_where)/select_n | solution.py:90
  204.7 15.4 %fusion.13 = f32[16,4,2,16,8]{0,3,4,2,1:T(8,128)S(1)} fusion(bf16[16,8,16,1024,1,1]{3,2,1,0,5,4:T(8,128)(2,1)} %bitcast.239, bf16[16,4,2,16,1024,1]{4,3,2,1,0,5:T(8,128)(2,1)} %bitcast.75), kind=kOutput, calls=%fused_computation.11 | convolution fusion | flops 536870912 | bytes 8454144 | tf_op jit(solution)/shard_map/dot_general | solution.py:102
  220.1 0.9 copy.118
  221.5 18.4 %all_to_all.24 = f32[64,1,256]{2,1,0:T(1,128)S(1)} all-to-all(f32[64,1,256]{2,1,0:T(1,128)S(1)} %all_to_all.20), channel_id=1, replica_groups={{0,2,4,6,8,10,12,14,16,18,20,22,24,26,28,30,32,34,36,38,40,42,44,46,48,..., dimensions={0} | all-to-all | bytes 131072 | tf_op jit(solution)/shard_map/all_to_all | solution.py:107
  240.3 1.1 collective-permute-done.18
  (98 shorter events, 19.3 us)
Async XLA Ops:
  1.8 23.5 %collective-permute-start.7 = (bf16[64,1024]{1,0:T(8,128)(2,1)S(1)}, bf16[64,1024]{1,0:T(8,128)(2,1)S(1)}, u32[]{:S(2)}, u32[]{:S(2)}) collective-permute-start(bf16[64,1024]{1,0:T(8,128)(2,1)S(1)} %bitcast_multiply_fusion), channel_id=1, source_target_pairs={{0,24},{8,0},{16,8},{24,16},{32,56},{40,32},{48,40},{56,48},{64,88... | collective-permute-start | bytes 393224 | tf_op jit(solution)/shard_map/ppermute | solution.py:37
  4.7 26.3 %collective-permute-start.6 = (bf16[64,1024]{1,0:T(8,128)(2,1)S(1)}, bf16[64,1024]{1,0:T(8,128)(2,1)S(1)}, u32[]{:S(2)}, u32[]{:S(2)}) collective-permute-start(bf16[64,1024]{1,0:T(8,128)(2,1)S(1)} %bitcast_multiply_fusion), channel_id=1, source_target_pairs={{0,8},{8,16},{16,24},{24,0},{32,40},{40,48},{48,56},{56,32},{64,72... | collective-permute-start | bytes 393224 | tf_op jit(solution)/shard_map/ppermute | solution.py:36
  5.8 22.5 %collective-permute-start.1 = (bf16[64,1024]{1,0:T(8,128)(2,1)S(1)}, bf16[64,1024]{1,0:T(8,128)(2,1)S(1)}, u32[]{:S(2)}, u32[]{:S(2)}) collective-permute-start(bf16[64,1024]{1,0:T(8,128)(2,1)S(1)} %bitcast_multiply_fusion.2), channel_id=1, source_target_pairs={{0,96},{8,104},{16,112},{24,120},{32,0},{40,8},{48,16},{56,24},{64... | collective-permute-start | bytes 393224 | tf_op jit(solution)/shard_map/ppermute | solution.py:37
  8.9 23.5 %collective-permute-start = (bf16[64,1024]{1,0:T(8,128)(2,1)S(1)}, bf16[64,1024]{1,0:T(8,128)(2,1)S(1)}, u32[]{:S(2)}, u32[]{:S(2)}) collective-permute-start(bf16[64,1024]{1,0:T(8,128)(2,1)S(1)} %bitcast_multiply_fusion.2), channel_id=1, source_target_pairs={{0,32},{8,40},{16,48},{24,56},{32,64},{40,72},{48,80},{56,88},{64,... | collective-permute-start | bytes 393224 | tf_op jit(solution)/shard_map/ppermute | solution.py:36
  12.8 8.5 %copy-start.4 = (bf16[2,64,1024]{2,1,0:T(8,128)(2,1)S(1)}, bf16[2,64,1024]{2,1,0:T(8,128)(2,1)}, u32[]{:S(2)}) copy-start(bf16[2,64,1024]{2,1,0:T(8,128)(2,1)} %param.8) | copy-start | bytes 786436
  12.8 9.2 %copy-start.5 = (bf16[2,64,1024]{2,1,0:T(8,128)(2,1)S(1)}, bf16[2,64,1024]{2,1,0:T(8,128)(2,1)}, u32[]{:S(2)}) copy-start(bf16[2,64,1024]{2,1,0:T(8,128)(2,1)} %param.7) | copy-start | bytes 786436
  12.8 63.8 %all-to-all-start = ((bf16[16,64,1024]{2,1,0:T(8,128)(2,1)}), bf16[16,64,1024]{2,1,0:T(8,128)(2,1)}, u32[]{:S(2)}, u32[]{:S(2)}) async-start(bf16[16,64,1024]{2,1,0:T(8,128)(2,1)} %broadcast_multiply_fusion), calls=%async_computation | async-start | bytes 4194304 | tf_op jit(solution)/shard_map/all_to_all | solution.py:72
  25.3 23.2 %collective-permute-start.8 = (bf16[64,1024]{1,0:T(8,128)(2,1)S(1)}, bf16[64,1024]{1,0:T(8,128)(2,1)S(1)}, u32[]{:S(2)}, u32[]{:S(2)}) collective-permute-start(bf16[64,1024]{1,0:T(8,128)(2,1)S(1)} %collective-permute-done.7), channel_id=1, source_target_pairs={{0,24},{8,0},{16,8},{24,16},{32,56},{40,32},{48,40},{56,48},{64,88... | collective-permute-start | bytes 393224 | tf_op jit(solution)/shard_map/ppermute | solution.py:38
  28.3 23.6 %collective-permute-start.2 = (bf16[64,1024]{1,0:T(8,128)(2,1)S(1)}, bf16[64,1024]{1,0:T(8,128)(2,1)S(1)}, u32[]{:S(2)}, u32[]{:S(2)}) collective-permute-start(bf16[64,1024]{1,0:T(8,128)(2,1)S(1)} %collective-permute-done.1), channel_id=1, source_target_pairs={{0,96},{8,104},{16,112},{24,120},{32,0},{40,8},{48,16},{56,24},{64... | collective-permute-start | bytes 393224 | tf_op jit(solution)/shard_map/ppermute | solution.py:38
  32.4 22.8 %copy-start.1 = (bf16[1,4,64,1024]{3,2,0,1:T(8,128)(2,1)}, bf16[1,4,64,1024]{3,2,0,1:T(8,128)(2,1)S(1)}, u32[]{:S(2)}) copy-start(bf16[1,4,64,1024]{3,2,0,1:T(8,128)(2,1)S(1)} %bitcast_dynamic-update-slice_fusion.5) | copy-start | bytes 1572868
  48.6 12.7 %collective-permute-start.9 = (bf16[256,1024]{1,0:T(8,128)(2,1)S(1)}, bf16[256,1024]{1,0:T(8,128)(2,1)S(1)}, u32[]{:S(2)}, u32[]{:S(2)}) collective-permute-start(bf16[256,1024]{1,0:T(8,128)(2,1)S(1)} %pad_maximum_fusion.4), channel_id=1, source_target_pairs={{0,32},{8,40},{16,48},{24,56},{32,64},{40,72},{48,80},{56,88},{64,... | collective-permute-start | bytes 1572872 | tf_op jit(solution)/shard_map/ppermute | solution.py:36
  49.3 12.1 %collective-permute-start.10 = (bf16[256,1024]{1,0:T(8,128)(2,1)S(1)}, bf16[256,1024]{1,0:T(8,128)(2,1)S(1)}, u32[]{:S(2)}, u32[]{:S(2)}) collective-permute-start(bf16[256,1024]{1,0:T(8,128)(2,1)S(1)} %pad_maximum_fusion.4), channel_id=1, source_target_pairs={{0,96},{8,104},{16,112},{24,120},{32,0},{40,8},{48,16},{56,24},{64... | collective-permute-start | bytes 1572872 | tf_op jit(solution)/shard_map/ppermute | solution.py:37
  51.9 12.4 %collective-permute-start.3 = (bf16[256,1024]{1,0:T(8,128)(2,1)S(1)}, bf16[256,1024]{1,0:T(8,128)(2,1)S(1)}, u32[]{:S(2)}, u32[]{:S(2)}) collective-permute-start(bf16[256,1024]{1,0:T(8,128)(2,1)S(1)} %pad_maximum_fusion.3), channel_id=1, source_target_pairs={{0,8},{8,16},{16,24},{24,0},{32,40},{40,48},{48,56},{56,32},{64,72... | collective-permute-start | bytes 1572872 | tf_op jit(solution)/shard_map/ppermute | solution.py:36
  53.5 12.5 %collective-permute-start.4 = (bf16[256,1024]{1,0:T(8,128)(2,1)S(1)}, bf16[256,1024]{1,0:T(8,128)(2,1)}, u32[]{:S(2)}, u32[]{:S(2)}) collective-permute-start(bf16[256,1024]{1,0:T(8,128)(2,1)S(1)} %pad_maximum_fusion.3), channel_id=1, source_target_pairs={{0,24},{8,0},{16,8},{24,16},{32,56},{40,32},{48,40},{56,48},{64,88... | collective-permute-start | bytes 1572872 | tf_op jit(solution)/shard_map/ppermute | solution.py:37
  55.9 1.4 copy-start.2
  61.4 11.6 %collective-permute-start.11 = (bf16[256,1024]{1,0:T(8,128)(2,1)S(1)}, bf16[256,1024]{1,0:T(8,128)(2,1)S(1)}, u32[]{:S(2)}, u32[]{:S(2)}) collective-permute-start(bf16[256,1024]{1,0:T(8,128)(2,1)S(1)} %collective-permute-done.10), channel_id=1, source_target_pairs={{0,96},{8,104},{16,112},{24,120},{32,0},{40,8},{48,16},{56,24},{64... | collective-permute-start | bytes 1572872 | tf_op jit(solution)/shard_map/ppermute | solution.py:38
  66.0 13.3 %collective-permute-start.5 = (bf16[256,1024]{1,0:T(8,128)(2,1)}, bf16[256,1024]{1,0:T(8,128)(2,1)}, u32[]{:S(2)}, u32[]{:S(2)}) collective-permute-start(bf16[256,1024]{1,0:T(8,128)(2,1)} %collective-permute-done.4), channel_id=1, source_target_pairs={{0,24},{8,0},{16,8},{24,16},{32,56},{40,32},{48,40},{56,48},{64,88... | collective-permute-start | bytes 1572872 | tf_op jit(solution)/shard_map/ppermute | solution.py:38
  76.6 15.6 %collective-permute-start.12 = (bf16[1024,1024]{1,0:T(8,128)(2,1)}, bf16[1024,1024]{1,0:T(8,128)(2,1)}, u32[]{:S(2)}, u32[]{:S(2)}) collective-permute-start(bf16[1024,1024]{1,0:T(8,128)(2,1)} %bitcast.35), channel_id=1, source_target_pairs={{0,1},{1,0},{2,3},{3,2},{4,5},{5,4},{6,7},{7,6},{8,9},{9,8},{10,11... | collective-permute-start | bytes 6291464 | tf_op jit(solution)/shard_map/ppermute | solution.py:73
  79.3 4.7 %copy-start = (bf16[4,4,64,1024]{3,2,1,0:T(8,128)(2,1)S(1)}, bf16[4,4,64,1024]{3,2,1,0:T(8,128)(2,1)}, u32[]{:S(2)}) copy-start(bf16[4,4,64,1024]{3,2,1,0:T(8,128)(2,1)} %copy.113) | copy-start | bytes 6291460
  104.8 13.4 %copy-start.3 = (bf16[8,16,1024]{2,1,0:T(8,128)(2,1)S(1)}, bf16[8,16,1024]{2,1,0:T(8,128)(2,1)}, u32[]{:S(2)}) copy-start(bf16[8,16,1024]{2,1,0:T(8,128)(2,1)} %get-tuple-element.7) | copy-start | bytes 786436
  104.8 99.9 %all-to-all-start.1 = ((bf16[64,2,16,1024]{3,2,1,0:T(8,128)(2,1)}), bf16[64,2,16,1024]{3,2,1,0:T(8,128)(2,1)}, u32[]{:S(2)}, u32[]{:S(2)}) async-start(bf16[64,2,16,1024]{3,2,1,0:T(8,128)(2,1)} %pad_maximum_fusion), calls=%async_computation.1 | async-start | bytes 8388608 | tf_op jit(solution)/shard_map/all_to_all | solution.py:99
  118.3 63.9 %collective-permute-start.14 = (bf16[24,16,1024]{2,1,0:T(8,128)(2,1)S(1)}, bf16[24,16,1024]{2,1,0:T(8,128)(2,1)}, u32[]{:S(2)}, u32[]{:S(2)}) collective-permute-start(bf16[24,16,1024]{2,1,0:T(8,128)(2,1)S(1)} %pad_maximum_fusion.2), channel_id=1, source_target_pairs={{0,6},{1,7},{2,0},{3,1},{4,2},{5,3},{6,4},{7,5},{8,14},{9,15},{10,... | collective-permute-start | bytes 2359304 | tf_op jit(solution)/shard_map/ppermute | solution.py:81
  122.0 63.7 %collective-permute-start.13 = (bf16[24,16,1024]{2,1,0:T(8,128)(2,1)}, bf16[24,16,1024]{2,1,0:T(8,128)(2,1)}, u32[]{:S(2)}, u32[]{:S(2)}) collective-permute-start(bf16[24,16,1024]{2,1,0:T(8,128)(2,1)} %pad_maximum_fusion.1), channel_id=1, source_target_pairs={{0,2},{1,3},{2,4},{3,5},{4,6},{5,7},{6,0},{7,1},{8,10},{9,11},{10,... | collective-permute-start | bytes 2359304 | tf_op jit(solution)/shard_map/ppermute | solution.py:80
  183.1 7.9 %collective-permute-start.16 = (bf16[8,16,1024]{2,1,0:T(8,128)(2,1)S(1)}, bf16[8,16,1024]{2,1,0:T(8,128)(2,1)S(1)}, u32[]{:S(2)}, u32[]{:S(2)}) collective-permute-start(bf16[8,16,1024]{2,1,0:T(8,128)(2,1)S(1)} %slice.118), channel_id=1, source_target_pairs={{0,6},{1,7},{2,0},{3,1},{4,2},{5,3},{6,4},{7,5},{8,14},{9,15},{10,... | collective-permute-start | bytes 786440 | tf_op jit(solution)/shard_map/ppermute | solution.py:85
  186.7 8.8 %collective-permute-start.15 = (bf16[8,16,1024]{2,1,0:T(8,128)(2,1)S(1)}, bf16[8,16,1024]{2,1,0:T(8,128)(2,1)S(1)}, u32[]{:S(2)}, u32[]{:S(2)}) collective-permute-start(bf16[8,16,1024]{2,1,0:T(8,128)(2,1)S(1)} %slice.117), channel_id=1, source_target_pairs={{0,2},{1,3},{2,4},{3,5},{4,6},{5,7},{6,0},{7,1},{8,10},{9,11},{10,... | collective-permute-start | bytes 786440 | tf_op jit(solution)/shard_map/ppermute | solution.py:84
  195.6 4.6 %collective-permute-start.17 = (bf16[4,16,16,1024]{3,2,1,0:T(8,128)(2,1)S(1)}, bf16[4,16,16,1024]{3,2,1,0:T(8,128)(2,1)}, u32[]{:S(2)}, u32[]{:S(2)}) collective-permute-start(bf16[4,16,16,1024]{3,2,1,0:T(8,128)(2,1)S(1)} %fusion.24), channel_id=1, source_target_pairs={{0,1},{1,0},{2,3},{3,2},{4,5},{5,4},{6,7},{7,6},{8,9},{9,8},{10,11... | collective-permute-start | bytes 6291464 | tf_op jit(solution)/shard_map/ppermute | solution.py:89
  240.1 1.2 collective-permute-start.18

commit v3 on v1

v3 whole, which is shorter than its diff:
```python
import jax
import jax.numpy as jnp
from jax import lax
from jax.experimental import pallas as pl
from jax.experimental.pallas import tpu as pltpu
from jax.sharding import PartitionSpec as P

ALL = ("ao", "aux")
SIDE = 4
CORES = 2
OFFSETS = (0, -1, 1, 2)
MIB = 1 << 20
LANES = 128

OTHER_CORE = [(k, k ^ 1) for k in range(SIDE * CORES)]
SAME_CORE = [
    [i * SIDE * CORES + CORES * z + core for i in range(SIDE * SIDE) for z in range(SIDE)]
    for core in range(CORES)
]


def expand(mask_row, width):
    return jnp.repeat(mask_row, width, axis=-1).astype(jnp.bfloat16)


def in_plane(step, swapped):
    pairs = []
    for i in range(SIDE * SIDE):
        x, y = i % SIDE, i // SIDE
        for k in range(SIDE * CORES):
            if (k % CORES == 1) != swapped:
                to = ((y + step) % SIDE) * SIDE + x
            else:
                to = y * SIDE + (x + step) % SIDE
            pairs.append((i * SIDE * CORES + k, to * SIDE * CORES + k))
    return pairs


def along_z(step):
    return [(k, ((k // CORES + step) % SIDE) * CORES + k % CORES) for k in range(SIDE * CORES)]


def ring(rows, swapped):
    before = lax.ppermute(rows, ALL, in_plane(1, swapped))
    after = lax.ppermute(rows, ALL, in_plane(-1, swapped))
    far = lax.ppermute(after, ALL, in_plane(-1, swapped))
    return rows, before, after, far


def hold(value, *others):
    def kernel(*refs):
        pass

    whole = pl.BlockSpec(memory_space=pl.ANY)
    return pl.pallas_call(
        kernel,
        out_shape=jax.ShapeDtypeStruct(value.shape, value.dtype),
        in_specs=[whole] * (1 + len(others)),
        out_specs=whole,
        input_output_aliases={0: 0},
    )(value, *others)


def occ_product(matrix, pieces, into, index):
    depth, width = matrix.shape
    chips, _, slab, _ = into if isinstance(into, tuple) else into.shape
    rows = depth // SIDE**2
    columns = width // 4
    first = isinstance(into, tuple)

    def kernel(matrix_ref, *refs):
        piece_refs, (out_ref, occ, sems) = refs[:SIDE], refs[-3:]

        @pl.when(pl.program_id(0) == 0)
        def _():
            spot = lax.axis_index("ao")
            core = lax.axis_index("aux") % CORES
            x, y = spot % SIDE, spot // SIDE
            outer, inner = jnp.where(core == 0, y, x), jnp.where(core == 0, x, y)
            outer_step, inner_step = jnp.where(core == 0, SIDE, 1), jnp.where(core == 0, 1, SIDE)
            copies = []
            for g in range(SIDE):
                for k in range(SIDE):
                    block = ((outer + OFFSETS[g] + SIDE) % SIDE) * outer_step
                    block += ((inner + OFFSETS[k] + SIDE) % SIDE) * inner_step
                    copies.append(
                        pltpu.make_async_copy(
                            piece_refs[g].at[pl.ds(k * rows, rows)],
                            occ.at[pl.ds(pl.multiple_of(block * rows, rows), rows)],
                            sems.at[g * SIDE + k],
                        )
                    )
            for copy in copies:
                copy.start()
            for copy in copies:
                copy.wait()

        product = jnp.dot(occ[...], matrix_ref[...], preferred_element_type=jnp.float32)
        out_ref[...] = product.astype(jnp.bfloat16).reshape(out_ref.shape)

    anywhere = pl.BlockSpec(memory_space=pl.ANY)
    shape = into if first else into.shape
    return pl.pallas_call(
        kernel,
        grid=(width // columns,),
        out_shape=jax.ShapeDtypeStruct(shape, jnp.bfloat16),
        in_specs=[pl.BlockSpec((depth, columns), lambda j: (0, j))]
        + [anywhere] * SIDE
        + ([] if first else [anywhere]),
        out_specs=pl.BlockSpec((chips, 1, slab, columns), lambda j: (0, index, 0, j)),
        scratch_shapes=[
            pltpu.VMEM((depth, width), jnp.bfloat16),
            pltpu.SemaphoreType.DMA((SIDE * SIDE,)),
        ],
        input_output_aliases={} if first else {1 + SIDE: 0},
        compiler_params=pltpu.CompilerParams(vmem_limit_bytes=40 * MIB),
        cost_estimate=pl.CostEstimate(
            flops=2 * depth * depth * width, bytes_accessed=6 * depth * width, transcendentals=0
        ),
    )(matrix, *pieces, *([] if first else [into]))


def final_product(got, other):
    sources, pair, slab, width = got.shape
    count = other.shape[-1]
    columns = width // 4

    def kernel(got_ref, other_ref, out_ref, wide):
        total = jnp.zeros(out_ref.shape, jnp.float32)
        for part in range(columns // LANES):
            lanes = pl.ds(part * LANES, LANES)
            wide[part] = got_ref[..., lanes].reshape(wide.shape[1:]).astype(jnp.float32)
        for row in range(slab):
            left = [wide[part, pl.ds(row, sources * pair, stride=slab), :] for part in range(columns // LANES)]
            left = jnp.concatenate(left, 1).astype(jnp.bfloat16)
            total += jnp.dot(left, other_ref[row], preferred_element_type=jnp.float32)

        @pl.when(pl.program_id(0) == 0)
        def _():
            out_ref[...] = jnp.zeros_like(out_ref)

        out_ref[...] += total

    return pl.pallas_call(
        kernel,
        grid=(width // columns,),
        out_shape=jax.ShapeDtypeStruct((sources * pair, count), jnp.float32),
        in_specs=[
            pl.BlockSpec((sources, pair, slab, columns), lambda j: (0, 0, 0, j)),
            pl.BlockSpec((slab, columns, count), lambda j: (0, j, 0)),
        ],
        out_specs=pl.BlockSpec((sources * pair, count), lambda j: (0, 0)),
        scratch_shapes=[pltpu.VMEM((columns // LANES, sources * pair * slab, LANES), jnp.float32)],
        compiler_params=pltpu.CompilerParams(vmem_limit_bytes=40 * MIB),
        cost_estimate=pl.CostEstimate(
            flops=2 * sources * pair * slab * width * count,
            bytes_accessed=2 * got.size + 2 * other.size,
            transcendentals=0,
        ),
    )(got, other)


def body(three_centre, tensor_mask, occ_density, virt_density, density_mask):
    per_group, rows, width = three_centre.shape
    chips = SIDE**3
    slab = width // chips
    z, core = lax.axis_index("aux") // CORES, lax.axis_index("aux") % CORES

    dens_mask = expand(density_mask[:, 0, :], rows)
    row_mask = expand(tensor_mask[0], rows)
    occ_rows = lax.dynamic_index_in_dim(occ_density, core, 0, False) * dens_mask[0][None, :]
    virt_rows = lax.dynamic_index_in_dim(virt_density, core, 0, False) * dens_mask[1][None, :]

    occ_line = jnp.concatenate(ring(occ_rows, False), 0)
    occ_pieces = ring(occ_line, True)

    def cut(offset):
        view = three_centre.reshape(per_group, SIDE, slab, width)
        return lax.dynamic_index_in_dim(view, (z + offset) % SIDE, 1, False) * row_mask

    far, cut_at = cut(2), per_group // 2
    before = lax.ppermute(jnp.concatenate([cut(1), far[:cut_at]]), "aux", along_z(1))
    after = lax.ppermute(jnp.concatenate([cut(3), far[cut_at:]]), "aux", along_z(-1))
    far_a = lax.ppermute(before[per_group:], "aux", along_z(1))
    far_b = lax.ppermute(after[per_group:], "aux", along_z(-1))

    screened = hold(three_centre * row_mask, *occ_pieces[1:], far_a, far_b)
    own = lax.all_to_all(screened, "ao", split_axis=0, concat_axis=1, tiled=True)[0]
    twin = lax.ppermute(own, "aux", OTHER_CORE)

    slabs = jnp.concatenate([cut(0), after[:per_group], far_a, far_b, before[:per_group]])
    slabs = jnp.roll(slabs.reshape(SIDE, per_group, slab, width), z, axis=0)
    slabs_twin = lax.ppermute(slabs, "aux", OTHER_CORE)

    products = occ_product(own, occ_pieces, (chips, CORES, slab, width), 0)
    products = hold(occ_product(twin, occ_pieces, products, 1), slabs_twin)
    got = lax.all_to_all(
        products, ALL, split_axis=0, concat_axis=0, tiled=True, axis_index_groups=SAME_CORE
    )

    virt = lax.all_gather(virt_rows, "ao", axis=0, tiled=True)
    tensor_slab = jnp.where(
        core == 0, jnp.stack([slabs, slabs_twin], 1), jnp.stack([slabs_twin, slabs], 1)
    ).reshape(-1, slab, width)
    other = lax.dot_general(
        tensor_slab, virt, (((2,), (1,)), ((), ())), preferred_element_type=jnp.float32
    ).astype(jnp.bfloat16)
    other = jnp.transpose(other, (1, 2, 0))

    part = final_product(got, other)
    part = part.reshape(SIDE * SIDE, SIDE, CORES, SIDE * SIDE, -1)
    parcels = jnp.transpose(part, (3, 1, 2, 0, 4)).reshape(chips, -1)
    summed = lax.all_to_all(
        parcels, ALL, split_axis=0, concat_axis=0, tiled=True, axis_index_groups=SAME_CORE
    ).sum(axis=0).reshape(CORES, per_group, -1)
    mine, theirs = summed[0], lax.ppermute(summed[1], "aux", OTHER_CORE)
    return jnp.where(core == 0, jnp.stack([mine, theirs]), jnp.stack([theirs, mine]))


def solution(mesh):
    return jax.shard_map(
        body,
        mesh=mesh,
        in_specs=(
            P("aux", "ao", None),
            P("ao", None),
            P(None, "ao", None),
            P(None, "ao", None),
            P(None, "ao", None),
        ),
        out_specs=P(None, "aux", "ao"),
        check_vma=False,
    )
```

time: 198 us -> 223 us (1.13)
  matrix products: 30.9 us -> 11.1 us
  Pallas kernels: 0 us -> 19.7 us
  local copies, waits for them, and re-layouts: 5.69 us -> 17.7 us
  waiting for transfers between devices: 97.6 us -> 86.4 us
  other arithmetic: 6.64 us -> 15 us
  starting transfers between devices: 28.9 us -> 36.5 us
  blocking collectives: 13.9 us -> 20.8 us
    all_to_all x3 -> x1, waiting for transfers between devices: 44.3 us -> 0.01 us  [body(): lax.all_to_all(products, ALL, split_axis=0, concat_axis=0, tiled=True, ax...]
    all_gather x1, waiting for transfers between devices: 19.1 us -> 48.4 us  [body(): virt = lax.all_gather(virt_rows, 'ao', axis=0, tiled=True)]
    ppermute x1 -> x13, starting transfers between devices: 0.51 us -> 23 us  [the longest x2 6.93 us: ring(): far = lax.ppermute(after, ALL, in_plane(-1, swapped))]
    dot_general x4 -> x1, matrix products: 30.9 us -> 11.1 us  [body(): lax.dot_general(tensor_slab, virt, (((2,), (1,)), ((), ())), preferred_el...]
    pallas_call x0 -> x5, Pallas kernels: none -> 19.7 us  [the longest x2 14.3 us: occ_product(): pl.pallas_call(kernel, grid=(width // columns,), out_shape=jax.ShapeDtype...]
    all_to_all x3 -> x1, starting transfers between devices: 21.1 us -> 7.08 us  [body(): lax.all_to_all(products, ALL, split_axis=0, concat_axis=0, tiled=True, ax...]
    ppermute x1 -> x13, waiting for transfers between devices: 0.01 us -> 11.5 us  [the longest x2 6.7 us: ring(): after = lax.ppermute(rows, ALL, in_plane(-1, swapped))]
    unnamed x2 -> x43, local copies, waits for them, and re-layouts: 0.01 us -> 11.1 us
  transfers between devices with their start and end apart: 6 -> 16, of which waited for: 4 -> 9; matrix products, arithmetic and copies ran while one was open for 15% -> 14% of each run, Pallas kernels for 0% -> 6%
where the time goes in v3:
time: 223 us; the launch traced here: 221 us
  waiting for transfers between devices  86.4 us (39%)
  starting transfers between devices  36.5 us (16%)
  blocking collectives  20.8 us (9%)
  Pallas kernels  19.7 us (9%)
  local copies, waits for them, and re-layouts  17.7 us (8%)
  other arithmetic  15 us (7%)
  between operations  13.7 us (6%)
  matrix products  11.1 us (5%)
    all_gather x1, waiting for transfers between devices, body(): virt = lax.all_gather(virt_rows, 'ao', axis=0, tiled=True)  48.4 us
    all_to_all x1, waiting for transfers between devices, body(): lax.all_to_all(screened, 'ao', split_axis=0, concat_axis=1, tiled=True)[0]  26.5 us
    all_to_all x1, blocking collectives, body(): lax.all_to_all(parcels, ALL, split_axis=0, concat_axis=0, tiled=True, axi...  20.8 us
    pallas_call x2, Pallas kernels, occ_product(): pl.pallas_call(kernel, grid=(width // columns,), out_shape=jax.ShapeDtype...  14.3 us
    unnamed x43, local copies, waits for them, and re-layouts  11.1 us
    dot_general x1, matrix products, body(): lax.dot_general(tensor_slab, virt, (((2,), (1,)), ((), ())), preferred_el...  11.1 us
    all_to_all x1, starting transfers between devices, body(): lax.all_to_all(products, ALL, split_axis=0, concat_axis=0, tiled=True, ax...  7.08 us
    ppermute x2, starting transfers between devices, ring(): far = lax.ppermute(after, ALL, in_plane(-1, swapped))  6.93 us
  transfers between devices with their start and end apart: 16, of which 9 were waited for; matrix products, arithmetic and copies ran while one was open for 14% of the time, Pallas kernels for 6%

profile of v3, /device:TPU:0, one launch (start us, length us, event | category | flops | bytes accessed | tf_op | source)
XLA Modules:
  0.0 220.9 jit_solution(16540877914958802063)
XLA Ops:
  6.5 0.7 convert_element_type.30
  7.4 0.9 bitcast_multiply_fusion.5
  8.3 2.9 %collective-permute-start.1 = (bf16[64,1024]{1,0:T(8,128)(2,1)S(1)}, bf16[64,1024]{1,0:T(8,128)(2,1)S(1)}, u32[]{:S(2)}, u32[]{:S(2)}) collective-permute-start(bf16[64,1024]{1,0:T(8,128)(2,1)S(1)} %bitcast_multiply_fusion.5), channel_id=1, source_target_pairs={{0,24},{1,97},{2,26},{3,99},{4,28},{5,101},{6,30},{7,103},{8,0},{9... | collective-permute-start | bytes 393224 | tf_op jit(solution)/shard_map/ppermute | solution.py:45
  11.2 0.7 convert_bitcast_fusion.1
  12.0 2.9 %fusion.6 = (bf16[64,16,1024]{2,1,0:T(8,128)(2,1)}, bf16[16,16,1024]{2,1,0:T(8,128)(2,1)S(1)}, bf16[16,16,1024]{2,1,0:T(8,128)(2,1)S(1)}, bf16[16,16,1024]{2,1,0:T(8,128)(2,1)S(1)}) fusion(bf16[16,4,16,1024]{3,2,1,0:T(8,128)(2,1)} %bitcast.48, s32[]{:T(128)S(6)} %select_n.86, bf16[1024]{0:T(1024)(128)(2,1)S(1)} %convert_element_type.29, s32[]{:T(128)S(6)} %select_n.84, ...), kind=kLoop, calls=%fused_computation.15 | loop fusion | flops 3407871 | bytes 4196368
  15.0 2.0 collective-permute-start.6
  17.0 3.2 %collective-permute-start.2 = (bf16[64,1024]{1,0:T(8,128)(2,1)S(1)}, bf16[64,1024]{1,0:T(8,128)(2,1)S(1)}, u32[]{:S(2)}, u32[]{:S(2)}) collective-permute-start(bf16[64,1024]{1,0:T(8,128)(2,1)S(1)} %collective-permute-done.1), channel_id=1, source_target_pairs={{0,24},{1,97},{2,26},{3,99},{4,28},{5,101},{6,30},{7,103},{8,0},{9... | collective-permute-start | bytes 393224 | tf_op jit(solution)/shard_map/ppermute | solution.py:46
  20.3 2.3 %collective-permute-start.8 = (bf16[24,16,1024]{2,1,0:T(8,128)(2,1)S(1)}, bf16[24,16,1024]{2,1,0:T(8,128)(2,1)S(1)}, u32[]{:S(2)}, u32[]{:S(2)}) collective-permute-start(bf16[24,16,1024]{2,1,0:T(8,128)(2,1)S(1)} %pad_maximum_fusion.1), channel_id=1, source_target_pairs={{0,6},{1,7},{2,0},{3,1},{4,2},{5,3},{6,4},{7,5},{8,14},{9,15},{10,... | collective-permute-start | bytes 2359304 | tf_op jit(solution)/shard_map/ppermute | solution.py:183
  22.8 3.1 %collective-permute-start.4 = (bf16[256,1024]{1,0:T(8,128)(2,1)S(1)}, bf16[256,1024]{1,0:T(8,128)(2,1)S(1)}, u32[]{:S(2)}, u32[]{:S(2)}) collective-permute-start(bf16[256,1024]{1,0:T(8,128)(2,1)S(1)} %pad_maximum_fusion.2.refs_0_), channel_id=1, source_target_pairs={{0,96},{1,25},{2,98},{3,27},{4,100},{5,29},{6,102},{7,31},{8,104},... | collective-permute-start | bytes 1572872 | tf_op jit(solution)/shard_map/ppermute | solution.py:45
  25.9 6.7 %collective-permute-done.4.refs_2_ = bf16[256,1024]{1,0:T(8,128)(2,1)S(1)} collective-permute-done((bf16[256,1024]{1,0:T(8,128)(2,1)S(1)}, bf16[256,1024]{1,0:T(8,128)(2,1)S(1)}, u32[]{:S(2)}, u32[]{:S(2)}) %collective-permute-start.4) | collective-permute-done | bytes 524320 | tf_op jit(solution)/shard_map/ppermute | solution.py:45
  32.6 3.7 %collective-permute-start.5 = (bf16[256,1024]{1,0:T(8,128)(2,1)S(1)}, bf16[256,1024]{1,0:T(8,128)(2,1)S(1)}, u32[]{:S(2)}, u32[]{:S(2)}) collective-permute-start(bf16[256,1024]{1,0:T(8,128)(2,1)S(1)} %collective-permute-done.4.refs_2_), channel_id=1, source_target_pairs={{0,96},{1,25},{2,98},{3,27},{4,100},{5,29},{6,102},{7,31},{8,104},... | collective-permute-start | bytes 1572872 | tf_op jit(solution)/shard_map/ppermute | solution.py:46
  36.3 0.4 collective-permute-done.6
  36.7 1.6 collective-permute-start.7
  38.3 0.7 collective-permute-done.8
  39.0 3.6 %collective-permute-start.9 = (bf16[8,16,1024]{2,1,0:T(8,128)(2,1)S(1)}, bf16[8,16,1024]{2,1,0:T(8,128)(2,1)S(1)}, u32[]{:S(2)}, u32[]{:S(2)}) collective-permute-start(bf16[8,16,1024]{2,1,0:T(8,128)(2,1)S(1)} %slice.77), channel_id=1, source_target_pairs={{0,6},{1,7},{2,0},{3,1},{4,2},{5,3},{6,4},{7,5},{8,14},{9,15},{10,... | collective-permute-start | bytes 786440 | tf_op jit(solution)/shard_map/ppermute | solution.py:185
  42.6 1.5 broadcast_multiply_fusion.refs_0_
  44.1 1.3 collective-permute-done.7.refs_4_
  45.4 1.2 collective-permute-done.9.refs_5_
  46.7 0.7 copy-done.16
  47.4 0.8 copy-done.5
  48.2 6.4 %all-to-all-start = ((bf16[16,64,1024]{2,1,0:T(8,128)(2,1)}), bf16[16,64,1024]{2,1,0:T(8,128)(2,1)S(1)}, u32[]{:S(2)}, u32[]{:S(2)}) async-start(bf16[16,64,1024]{2,1,0:T(8,128)(2,1)} %shard_map.55), calls=%async_computation | async-start | bytes 4194304 | tf_op jit(solution)/shard_map/all_to_all | solution.py:188
  54.7 1.9 slice_dynamic-update-slice_fusion.1
  56.6 0.7 constant_dynamic-update-slice_fusion.1
  57.3 0.8 constant_dynamic-update-slice_fusion
  58.1 26.5 %all-to-all-done = bf16[16,64,1024]{2,1,0:T(8,128)(2,1)S(1)} async-done(((bf16[16,64,1024]{2,1,0:T(8,128)(2,1)}), bf16[16,64,1024]{2,1,0:T(8,128)(2,1)S(1)}, u32[]{:S(2)}, u32[]{:S(2)}) %all-to-all-start) | async-done | bytes 2097184 | tf_op jit(solution)/shard_map/all_to_all | solution.py:188
  84.6 0.9 slice_dynamic-update-slice_fusion
  85.5 3.8 %fusion.4 = bf16[4,16,16,1024]{3,2,1,0:T(8,128)(2,1)} fusion(s32[]{:T(128)S(6)} %select_n.87, bf16[4,16,16,1024]{3,2,1,0:T(8,128)(2,1)} %bitcast.46), kind=kLoop, calls=%fused_computation.6 | loop fusion | flops 1048576 | bytes 4194308 | tf_op jit(solution)/shard_map/jit(_roll_dynamic)/concatenate | solution.py:192
  89.2 0.5 collective-permute-start.11
  89.9 0.7 bitcast_multiply_fusion.4
  90.6 1.0 copy-done.6
  91.7 1.0 copy-done.9
  92.7 6.7 %shard_map.56.refs_4_ = bf16[64,2,16,1024]{3,2,1,0:T(8,128)(2,1)S(1)} custom-call(bf16[1024,1024]{1,0:T(8,128)(2,1)S(1)} %bitcast.45, bf16[256,1024]{1,0:T(8,128)(2,1)S(1)} %copy-done.9, bf16[256,1024]{1,0:T(8,128)(2,1)S(1)} %copy-done.4, bf16[256,1024]{1,0:T(8,128)(2,1)S(1)} %copy-done.2, bf16[256,1024]{1,0:T(8,128)(2,1)S(1)} %copy-done.6), custom_call_target="tpu_custom_call" | custom-call | flops 2147483648 | bytes 6291456 | tf_op jit(solution)/shard_map/pallas_call | solution.py:103
  99.5 7.6 %shard_map.57.refs_0_ = bf16[64,2,16,1024]{3,2,1,0:T(8,128)(2,1)S(1)} custom-call(bf16[1024,1024]{1,0:T(8,128)(2,1)} %collective-permute-done.10.matrix_ref, bf16[256,1024]{1,0:T(8,128)(2,1)S(1)} %copy-done.10, bf16[256,1024]{1,0:T(8,128)(2,1)S(1)} %copy-done.4, bf16[256,1024]{1,0:T(8,128)(2,1)S(1)} %copy-done.2, ...), custom_call_target="tpu_custom_call", output_to_operand_aliasing={{}: (5, {})} | custom-call | flops 2147483648 | bytes 6291456 | tf_op jit(solution)/shard_map/pallas_call | solution.py:103
  107.1 1.9 copy-done
  109.1 7.1 %all-to-all-start.1 = ((bf16[64,2,16,1024]{3,2,1,0:T(8,128)(2,1)}), bf16[64,2,16,1024]{3,2,1,0:T(8,128)(2,1)}, u32[]{:S(2)}, u32[]{:S(2)}) async-start(bf16[64,2,16,1024]{3,2,1,0:T(8,128)(2,1)} %shard_map.58), calls=%async_computation.1 | async-start | bytes 8388608 | tf_op jit(solution)/shard_map/all_to_all | solution.py:197
  116.2 0.8 fusion.9
  116.9 2.9 %maximum_select_fusion = bf16[4,2,16,16,1024]{4,3,2,0,1:T(8,128)(2,1)S(1)} fusion(bf16[4,1,16,16,1024]{4,3,2,0,1:T(8,128)(2,1)} %bitcast.11, bf16[4,1,16,16,1024]{4,3,2,0,1:T(8,128)(2,1)S(1)} %fusion.9, pred[]{:T(512)S(6)} %eq.13), kind=kLoop, calls=%fused_computation.2 | loop fusion | flops 6291456 | bytes 8388609 | tf_op jit(solution)/shard_map/jit(_where)/select_n | solution.py:202
  119.8 2.5 %copy.34 = bf16[4,2,16,16,1024]{4,3,2,1,0:T(8,128)(2,1)} copy(bf16[4,2,16,16,1024]{4,3,2,0,1:T(8,128)(2,1)S(1)} %maximum_select_fusion) | data formatting | bytes 8388608 | tf_op jit(solution)/shard_map/jit(_where)/select_n | solution.py:202
  122.3 48.4 %all-gather.2.cloned.1.call-done = bf16[1024,1024]{1,0:T(8,128)(2,1)} async-done(((bf16[64,1024]{1,0:T(8,128)(2,1)}), bf16[1024,1024]{1,0:T(8,128)(2,1)}) %all-gather.2.cloned.1.call-update) | async-done | bytes 2097168 | tf_op jit(solution)/shard_map/all_gather | solution.py:201
  170.7 11.1 %convert_bitcast_fusion.other_ref = bf16[16,1024,128]{2,1,0:T(8,128)(2,1)} fusion(bf16[128,16,1024]{2,1,0:T(8,128)(2,1)} %bitcast.49, bf16[1024,1024]{1,0:T(8,128)(2,1)} %all-gather.2.cloned.1.call-done), kind=kOutput, calls=%fused_computation.5 | convolution fusion | flops 4297064448 | bytes 10485760 | tf_op jit(solution)/shard_map/dot_general | solution.py:205
  181.8 2.2 copy-done.11
  183.9 5.4 %shard_map.59 = f32[128,128]{1,0:T(8,128)S(1)} custom-call(bf16[64,2,16,1024]{3,2,1,0:T(8,128)(2,1)} %all-to-all-done.1.got_ref, bf16[16,1024,128]{2,1,0:T(8,128)(2,1)S(1)} %copy-done.11), custom_call_target="tpu_custom_call" | custom-call | flops 536870912 | bytes 8388608 | tf_op jit(solution)/shard_map/pallas_call | solution.py:144
  189.3 0.6 reshape.68
  189.9 0.6 copy.37
  190.5 0.5 all_to_all.20
  191.0 20.8 %all_to_all.24 = f32[64,1,256]{2,1,0:T(1,128)S(1)} all-to-all(f32[64,1,256]{2,1,0:T(1,128)S(1)} %all_to_all.20), channel_id=1, replica_groups={{0,2,4,6,8,10,12,14,16,18,20,22,24,26,28,30,32,34,36,38,40,42,44,46,48,..., dimensions={0} | all-to-all | bytes 131072 | tf_op jit(solution)/shard_map/all_to_all | solution.py:213
  212.2 1.1 collective-permute-done.12
  213.4 0.7 copy.42
  (70 shorter events, 1.5 us)
Async XLA Ops:
  8.3 8.7 %collective-permute-start.1 = (bf16[64,1024]{1,0:T(8,128)(2,1)S(1)}, bf16[64,1024]{1,0:T(8,128)(2,1)S(1)}, u32[]{:S(2)}, u32[]{:S(2)}) collective-permute-start(bf16[64,1024]{1,0:T(8,128)(2,1)S(1)} %bitcast_multiply_fusion.5), channel_id=1, source_target_pairs={{0,24},{1,97},{2,26},{3,99},{4,28},{5,101},{6,30},{7,103},{8,0},{9... | collective-permute-start | bytes 393224 | tf_op jit(solution)/shard_map/ppermute | solution.py:45
  11.2 11.4 %collective-permute-start = (bf16[64,1024]{1,0:T(8,128)(2,1)S(1)}, bf16[64,1024]{1,0:T(8,128)(2,1)S(1)}, u32[]{:S(2)}, u32[]{:S(2)}) collective-permute-start(bf16[64,1024]{1,0:T(8,128)(2,1)S(1)} %bitcast_multiply_fusion.5), channel_id=1, source_target_pairs={{0,8},{1,33},{2,10},{3,35},{4,12},{5,37},{6,14},{7,39},{8,16},{9,4... | collective-permute-start | bytes 393224 | tf_op jit(solution)/shard_map/ppermute | solution.py:44
  15.0 27.6 %copy-start.13 = (bf16[16,64,1024]{2,1,0:T(8,128)(2,1)S(1)}, bf16[16,64,1024]{2,1,0:T(8,128)(2,1)}, u32[]{:S(2)}) copy-start(bf16[16,64,1024]{2,1,0:T(8,128)(2,1)} %param.5) | copy-start | bytes 6291460
  15.0 21.6 %collective-permute-start.6 = (bf16[24,16,1024]{2,1,0:T(8,128)(2,1)S(1)}, bf16[24,16,1024]{2,1,0:T(8,128)(2,1)S(1)}, u32[]{:S(2)}, u32[]{:S(2)}) collective-permute-start(bf16[24,16,1024]{2,1,0:T(8,128)(2,1)S(1)} %pad_maximum_fusion), channel_id=1, source_target_pairs={{0,2},{1,3},{2,4},{3,5},{4,6},{5,7},{6,0},{7,1},{8,10},{9,11},{10,... | collective-permute-start | bytes 2359304 | tf_op jit(solution)/shard_map/ppermute | solution.py:182
  17.0 5.8 %collective-permute-start.2 = (bf16[64,1024]{1,0:T(8,128)(2,1)S(1)}, bf16[64,1024]{1,0:T(8,128)(2,1)S(1)}, u32[]{:S(2)}, u32[]{:S(2)}) collective-permute-start(bf16[64,1024]{1,0:T(8,128)(2,1)S(1)} %collective-permute-done.1), channel_id=1, source_target_pairs={{0,24},{1,97},{2,26},{3,99},{4,28},{5,101},{6,30},{7,103},{8,0},{9... | collective-permute-start | bytes 393224 | tf_op jit(solution)/shard_map/ppermute | solution.py:46
  20.3 18.7 %collective-permute-start.8 = (bf16[24,16,1024]{2,1,0:T(8,128)(2,1)S(1)}, bf16[24,16,1024]{2,1,0:T(8,128)(2,1)S(1)}, u32[]{:S(2)}, u32[]{:S(2)}) collective-permute-start(bf16[24,16,1024]{2,1,0:T(8,128)(2,1)S(1)} %pad_maximum_fusion.1), channel_id=1, source_target_pairs={{0,6},{1,7},{2,0},{3,1},{4,2},{5,3},{6,4},{7,5},{8,14},{9,15},{10,... | collective-permute-start | bytes 2359304 | tf_op jit(solution)/shard_map/ppermute | solution.py:183
  22.8 21.3 %copy-start.8 = (bf16[256,1024]{1,0:T(8,128)(2,1)}, bf16[256,1024]{1,0:T(8,128)(2,1)S(1)}, u32[]{:S(2)}) copy-start(bf16[256,1024]{1,0:T(8,128)(2,1)S(1)} %pad_maximum_fusion.2.refs_0_) | copy-start | bytes 1572868
  22.8 9.8 %collective-permute-start.4 = (bf16[256,1024]{1,0:T(8,128)(2,1)S(1)}, bf16[256,1024]{1,0:T(8,128)(2,1)S(1)}, u32[]{:S(2)}, u32[]{:S(2)}) collective-permute-start(bf16[256,1024]{1,0:T(8,128)(2,1)S(1)} %pad_maximum_fusion.2.refs_0_), channel_id=1, source_target_pairs={{0,96},{1,25},{2,98},{3,27},{4,100},{5,29},{6,102},{7,31},{8,104},... | collective-permute-start | bytes 1572872 | tf_op jit(solution)/shard_map/ppermute | solution.py:45
  25.9 18.2 %collective-permute-start.3 = (bf16[256,1024]{1,0:T(8,128)(2,1)S(1)}, bf16[256,1024]{1,0:T(8,128)(2,1)S(1)}, u32[]{:S(2)}, u32[]{:S(2)}) collective-permute-start(bf16[256,1024]{1,0:T(8,128)(2,1)S(1)} %pad_maximum_fusion.2.refs_0_), channel_id=1, source_target_pairs={{0,32},{1,9},{2,34},{3,11},{4,36},{5,13},{6,38},{7,15},{8,40},{9,1... | collective-permute-start | bytes 1572872 | tf_op jit(solution)/shard_map/ppermute | solution.py:44
  32.6 11.5 %copy-start.1 = (bf16[256,1024]{1,0:T(8,128)(2,1)}, bf16[256,1024]{1,0:T(8,128)(2,1)S(1)}, u32[]{:S(2)}) copy-start(bf16[256,1024]{1,0:T(8,128)(2,1)S(1)} %collective-permute-done.4.refs_2_) | copy-start | bytes 1572868
  32.6 14.1 %collective-permute-start.5 = (bf16[256,1024]{1,0:T(8,128)(2,1)S(1)}, bf16[256,1024]{1,0:T(8,128)(2,1)S(1)}, u32[]{:S(2)}, u32[]{:S(2)}) collective-permute-start(bf16[256,1024]{1,0:T(8,128)(2,1)S(1)} %collective-permute-done.4.refs_2_), channel_id=1, source_target_pairs={{0,96},{1,25},{2,98},{3,27},{4,100},{5,29},{6,102},{7,31},{8,104},... | collective-permute-start | bytes 1572872 | tf_op jit(solution)/shard_map/ppermute | solution.py:46
  36.7 8.7 %collective-permute-start.7 = (bf16[8,16,1024]{2,1,0:T(8,128)(2,1)S(1)}, bf16[8,16,1024]{2,1,0:T(8,128)(2,1)S(1)}, u32[]{:S(2)}, u32[]{:S(2)}) collective-permute-start(bf16[8,16,1024]{2,1,0:T(8,128)(2,1)S(1)} %slice.75), channel_id=1, source_target_pairs={{0,2},{1,3},{2,4},{3,5},{4,6},{5,7},{6,0},{7,1},{8,10},{9,11},{10,... | collective-permute-start | bytes 786440 | tf_op jit(solution)/shard_map/ppermute | solution.py:184
  39.0 5.1 %copy-start.18 = (bf16[24,16,1024]{2,1,0:T(8,128)(2,1)}, bf16[24,16,1024]{2,1,0:T(8,128)(2,1)S(1)}, u32[]{:S(2)}) copy-start(bf16[24,16,1024]{2,1,0:T(8,128)(2,1)S(1)} %collective-permute-done.8) | copy-start | bytes 2359300
  39.0 7.6 %collective-permute-start.9 = (bf16[8,16,1024]{2,1,0:T(8,128)(2,1)S(1)}, bf16[8,16,1024]{2,1,0:T(8,128)(2,1)S(1)}, u32[]{:S(2)}, u32[]{:S(2)}) collective-permute-start(bf16[8,16,1024]{2,1,0:T(8,128)(2,1)S(1)} %slice.77), channel_id=1, source_target_pairs={{0,6},{1,7},{2,0},{3,1},{4,2},{5,3},{6,4},{7,5},{8,14},{9,15},{10,... | collective-permute-start | bytes 786440 | tf_op jit(solution)/shard_map/ppermute | solution.py:185
  44.1 2.6 %copy-start.3 = (bf16[256,1024]{1,0:T(8,128)(2,1)}, bf16[256,1024]{1,0:T(8,128)(2,1)S(1)}, u32[]{:S(2)}) copy-start(bf16[256,1024]{1,0:T(8,128)(2,1)S(1)} %collective-permute-done.3.refs_1_) | copy-start | bytes 1572868
  45.4 1.3 copy-start.14
  46.7 0.7 copy-start.16
  47.4 0.8 copy-start.5
  48.2 8.4 %copy-start.15 = (bf16[8,16,1024]{2,1,0:T(8,128)(2,1)S(1)}, bf16[8,16,1024]{2,1,0:T(8,128)(2,1)}, u32[]{:S(2)}) copy-start(bf16[8,16,1024]{2,1,0:T(8,128)(2,1)} %copy-done.14) | copy-start | bytes 786436
  48.2 9.1 %copy-start.17 = (bf16[8,16,1024]{2,1,0:T(8,128)(2,1)S(1)}, bf16[8,16,1024]{2,1,0:T(8,128)(2,1)}, u32[]{:S(2)}) copy-start(bf16[8,16,1024]{2,1,0:T(8,128)(2,1)} %copy-done.16) | copy-start | bytes 786436
  48.2 36.4 %all-to-all-start = ((bf16[16,64,1024]{2,1,0:T(8,128)(2,1)}), bf16[16,64,1024]{2,1,0:T(8,128)(2,1)S(1)}, u32[]{:S(2)}, u32[]{:S(2)}) async-start(bf16[16,64,1024]{2,1,0:T(8,128)(2,1)} %shard_map.55), calls=%async_computation | async-start | bytes 4194304 | tf_op jit(solution)/shard_map/all_to_all | solution.py:188
  54.6 116.0 %all-gather.2.cloned.1.call-start = ((), (), s32[]{:S(2)}) async-start(), calls=%async_computation.3 | async-start | bytes 2228224 | tf_op jit(solution)/shard_map/all_gather | solution.py:201
  84.6 14.9 %collective-permute-start.10 = (bf16[1024,1024]{1,0:T(8,128)(2,1)S(1)}, bf16[1024,1024]{1,0:T(8,128)(2,1)}, u32[]{:S(2)}, u32[]{:S(2)}) collective-permute-start(bf16[1024,1024]{1,0:T(8,128)(2,1)S(1)} %bitcast.44), channel_id=1, source_target_pairs={{0,1},{1,0},{2,3},{3,2},{4,5},{5,4},{6,7},{7,6},{8,9},{9,8},{10,11... | collective-permute-start | bytes 6291464 | tf_op jit(solution)/shard_map/ppermute | solution.py:189
  85.5 4.5 %copy-start.19 = (bf16[2,64,1024]{2,1,0:T(8,128)(2,1)S(1)}, bf16[2,64,1024]{2,1,0:T(8,128)(2,1)}, u32[]{:S(2)}) copy-start(bf16[2,64,1024]{2,1,0:T(8,128)(2,1)} %param.8) | copy-start | bytes 786436
  85.5 5.1 %copy-start.2 = (bf16[256,1024]{1,0:T(8,128)(2,1)S(1)}, bf16[256,1024]{1,0:T(8,128)(2,1)}, u32[]{:S(2)}) copy-start(bf16[256,1024]{1,0:T(8,128)(2,1)} %copy-done.1) | copy-start | bytes 1572868
  85.5 5.2 %copy-start.4 = (bf16[256,1024]{1,0:T(8,128)(2,1)S(1)}, bf16[256,1024]{1,0:T(8,128)(2,1)}, u32[]{:S(2)}) copy-start(bf16[256,1024]{1,0:T(8,128)(2,1)} %copy-done.3) | copy-start | bytes 1572868
  89.2 19.8 %collective-permute-start.11 = (bf16[4,16,16,1024]{3,2,1,0:T(8,128)(2,1)}, bf16[4,16,16,1024]{3,2,1,0:T(8,128)(2,1)}, u32[]{:S(2)}, u32[]{:S(2)}) collective-permute-start(bf16[4,16,16,1024]{3,2,1,0:T(8,128)(2,1)} %fusion.4), channel_id=1, source_target_pairs={{0,1},{1,0},{2,3},{3,2},{4,5},{5,4},{6,7},{7,6},{8,9},{9,8},{10,11... | collective-permute-start | bytes 6291464 | tf_op jit(solution)/shard_map/ppermute | solution.py:193
  90.6 1.0 copy-start.6
  91.7 1.0 copy-start.9
  92.7 6.7 %copy-start.7 = (bf16[256,1024]{1,0:T(8,128)(2,1)S(1)}, bf16[256,1024]{1,0:T(8,128)(2,1)}, u32[]{:S(2)}) copy-start(bf16[256,1024]{1,0:T(8,128)(2,1)} %copy-done.5) | copy-start | bytes 1572868
  92.7 6.7 %copy-start.10 = (bf16[256,1024]{1,0:T(8,128)(2,1)S(1)}, bf16[256,1024]{1,0:T(8,128)(2,1)}, u32[]{:S(2)}) copy-start(bf16[256,1024]{1,0:T(8,128)(2,1)} %copy-done.8) | copy-start | bytes 1572868
  107.1 1.9 copy-start
  109.1 7.1 %copy-start.12 = (bf16[64,16,1024]{2,1,0:T(8,128)(2,1)S(1)}, bf16[64,16,1024]{2,1,0:T(8,128)(2,1)}, u32[]{:S(2)}) copy-start(bf16[64,16,1024]{2,1,0:T(8,128)(2,1)} %slice_dynamic-update-slice_fusion) | copy-start | bytes 6291460
  109.1 72.7 %all-to-all-start.1 = ((bf16[64,2,16,1024]{3,2,1,0:T(8,128)(2,1)}), bf16[64,2,16,1024]{3,2,1,0:T(8,128)(2,1)}, u32[]{:S(2)}, u32[]{:S(2)}) async-start(bf16[64,2,16,1024]{3,2,1,0:T(8,128)(2,1)} %shard_map.58), calls=%async_computation.1 | async-start | bytes 8388608 | tf_op jit(solution)/shard_map/all_to_all | solution.py:197
  181.8 2.2 copy-start.11
  212.0 1.2 collective-permute-start.12
Sparse Core Ops, SparseCore 0:
  90.7 79.8 all-gather.1

commit v4 on v3

v4 whole, which is shorter than its diff:
```python
import jax
import jax.numpy as jnp
from jax import lax
from jax.experimental import pallas as pl
from jax.experimental.pallas import tpu as pltpu
from jax.sharding import PartitionSpec as P

ALL = ("ao", "aux")
SIDE = 4
CORES = 2
MIB = 1 << 20
LANES = 128

OTHER_CORE = [(k, k ^ 1) for k in range(SIDE * CORES)]
SAME_CORE = [
    [i * SIDE * CORES + CORES * z + core for i in range(SIDE * SIDE) for z in range(SIDE)]
    for core in range(CORES)
]


def expand(mask_row, width):
    return jnp.repeat(mask_row, width, axis=-1).astype(jnp.bfloat16)


def hold(value, *others):
    def kernel(*refs):
        pass

    whole = pl.BlockSpec(memory_space=pl.ANY)
    return pl.pallas_call(
        kernel,
        out_shape=jax.ShapeDtypeStruct(value.shape, value.dtype),
        in_specs=[whole] * (1 + len(others)),
        out_specs=whole,
        input_output_aliases={0: 0},
    )(value, *others)


def occ_product(occ, matrix, into, index, *others):
    depth, width = matrix.shape
    first = isinstance(into, tuple)
    shape = into if first else into.shape
    columns = width // 2

    def kernel(occ_ref, matrix_ref, *refs):
        product = jnp.dot(occ_ref[0], matrix_ref[...], preferred_element_type=jnp.float32)
        refs[-1][...] = product.astype(jnp.bfloat16).reshape(refs[-1].shape)

    return pl.pallas_call(
        kernel,
        grid=(width // columns,),
        out_shape=jax.ShapeDtypeStruct(shape, jnp.bfloat16),
        in_specs=[
            pl.BlockSpec((1, depth, depth), lambda j: (0, 0, 0)),
            pl.BlockSpec((depth, columns), lambda j: (0, j)),
        ]
        + [pl.BlockSpec(memory_space=pl.ANY)] * (len(others) + (not first)),
        out_specs=pl.BlockSpec((shape[0], 1, shape[2], columns), lambda j: (0, index, 0, j)),
        input_output_aliases={} if first else {2: 0},
        compiler_params=pltpu.CompilerParams(vmem_limit_bytes=56 * MIB),
        cost_estimate=pl.CostEstimate(
            flops=2 * depth * depth * width, bytes_accessed=6 * depth * width, transcendentals=0
        ),
    )(occ, matrix, *([] if first else [into]), *others)


def final_product(got, other):
    sources, pair, slab, width = got.shape
    count = other.shape[-1]
    columns = width // 4

    def kernel(got_ref, other_ref, out_ref, wide):
        total = jnp.zeros(out_ref.shape, jnp.float32)
        for part in range(columns // LANES):
            lanes = pl.ds(part * LANES, LANES)
            wide[part] = got_ref[..., lanes].reshape(wide.shape[1:]).astype(jnp.float32)
        for row in range(slab):
            left = [wide[part, pl.ds(row, sources * pair, stride=slab), :] for part in range(columns // LANES)]
            left = jnp.concatenate(left, 1).astype(jnp.bfloat16)
            total += jnp.dot(left, other_ref[row], preferred_element_type=jnp.float32)

        @pl.when(pl.program_id(0) == 0)
        def _():
            out_ref[...] = jnp.zeros_like(out_ref)

        out_ref[...] += total

    return pl.pallas_call(
        kernel,
        grid=(width // columns,),
        out_shape=jax.ShapeDtypeStruct((sources * pair, count), jnp.float32),
        in_specs=[
            pl.BlockSpec((sources, pair, slab, columns), lambda j: (0, 0, 0, j)),
            pl.BlockSpec((slab, columns, count), lambda j: (0, j, 0)),
        ],
        out_specs=pl.BlockSpec((sources * pair, count), lambda j: (0, 0)),
        scratch_shapes=[pltpu.VMEM((columns // LANES, sources * pair * slab, LANES), jnp.float32)],
        compiler_params=pltpu.CompilerParams(vmem_limit_bytes=56 * MIB),
        cost_estimate=pl.CostEstimate(
            flops=2 * sources * pair * slab * width * count,
            bytes_accessed=2 * got.size + 2 * other.size,
            transcendentals=0,
        ),
    )(got, other)


def body(three_centre, tensor_mask, occ_density, virt_density, density_mask):
    per_group, rows, width = three_centre.shape
    chips = SIDE**3
    slab = width // chips
    core = lax.axis_index("aux") % CORES

    dens_mask = expand(density_mask[:, 0, :], rows)
    row_mask = expand(tensor_mask[0], rows)

    occ_rows = lax.dynamic_index_in_dim(occ_density, core, 0, False) * dens_mask[0][None, :]
    virt_rows = lax.dynamic_index_in_dim(virt_density, core, 0, False) * dens_mask[1][None, :]
    dens = lax.all_gather(jnp.stack([occ_rows, virt_rows]), "ao", axis=1, tiled=True)
    occ, virt = dens[0], dens[1]

    screened = three_centre * row_mask
    own = lax.all_to_all(screened, "ao", split_axis=0, concat_axis=1, tiled=True)[0]
    twin = lax.ppermute(own, "aux", OTHER_CORE)
    groups = lax.axis_size("aux")
    slabs = lax.all_to_all(
        screened.reshape(per_group, groups, -1, width), "aux", split_axis=1, concat_axis=0, tiled=True
    ).reshape(groups * per_group, -1, width)
    slabs_other = lax.ppermute(slabs, "aux", OTHER_CORE)

    products = occ_product(dens, own, (chips, CORES, slab, width), 0)
    products = occ_product(dens, twin, products, 1)
    products = hold(products, slabs)
    got = lax.all_to_all(
        products, ALL, split_axis=0, concat_axis=0, tiled=True, axis_index_groups=SAME_CORE
    )
    tensor_slab = jnp.where(
        core == 0, jnp.concatenate([slabs, slabs_other], 1), jnp.concatenate([slabs_other, slabs], 1)
    )
    other = lax.dot_general(
        tensor_slab, virt, (((2,), (1,)), ((), ())), preferred_element_type=jnp.float32
    ).astype(jnp.bfloat16)
    other = jnp.transpose(other, (1, 2, 0))

    part = final_product(got, other)
    part = part.reshape(SIDE * SIDE, SIDE, CORES, SIDE * SIDE, -1)
    parcels = jnp.transpose(part, (3, 1, 2, 0, 4)).reshape(chips, -1)
    summed = lax.all_to_all(
        parcels, ALL, split_axis=0, concat_axis=0, tiled=True, axis_index_groups=SAME_CORE
    ).sum(axis=0).reshape(CORES, per_group, -1)
    mine, theirs = summed[0], lax.ppermute(summed[1], "aux", OTHER_CORE)
    return jnp.where(core == 0, jnp.stack([mine, theirs]), jnp.stack([theirs, mine]))


def solution(mesh):
    return jax.shard_map(
        body,
        mesh=mesh,
        in_specs=(
            P("aux", "ao", None),
            P("ao", None),
            P(None, "ao", None),
            P(None, "ao", None),
            P(None, "ao", None),
        ),
        out_specs=P(None, "aux", "ao"),
        check_vma=False,
    )
```

time: 223 us -> 192 us (0.86)
  blocking collectives: 20.8 us -> 59.6 us
  waiting for transfers between devices: 86.4 us -> 55.7 us
  starting transfers between devices: 36.5 us -> 14.9 us
  local copies, waits for them, and re-layouts: 17.7 us -> 6.85 us
  other arithmetic: 15 us -> 9.73 us
    all_to_all x0 -> x1, blocking collectives: none -> 39.6 us  [body(): lax.all_to_all(screened, 'ao', split_axis=0, concat_axis=1, tiled=True)[0]]
    all_to_all x1, waiting for transfers between devices: 0.01 us -> 30.8 us  [body(): lax.all_to_all(products, ALL, split_axis=0, concat_axis=0, tiled=True, ax...]
    all_gather x1, waiting for transfers between devices: 48.4 us -> 19.5 us  [body(): lax.all_gather(jnp.stack([occ_rows, virt_rows]), 'ao', axis=1, tiled=True)]
    all_to_all x1, waiting for transfers between devices: 26.5 us -> 0.01 us  [body(): lax.all_to_all(screened.reshape(per_group, groups, -1, width), 'aux', spl...]
    ppermute x11 -> x1, starting transfers between devices: 22.9 us -> 0.27 us  [body(): slabs_other = lax.ppermute(slabs, 'aux', OTHER_CORE)]
    unnamed x43 -> x8, local copies, waits for them, and re-layouts: 11.1 us -> 1.33 us
    ppermute x11 -> x1, waiting for transfers between devices: 10.4 us -> 4.26 us  [body(): slabs_other = lax.ppermute(slabs, 'aux', OTHER_CORE)]
    concatenate x4 -> x0, other arithmetic: 3.95 us -> none  [the longest x1 3.78 us: body(): slabs = jnp.roll(slabs.reshape(SIDE, per_group, slab, width), z, axis=0)]
  transfers between devices with their start and end apart: 16 -> 6, of which waited for: 9 -> 4; matrix products, arithmetic and copies ran while one was open for 14% -> 11% of each run, Pallas kernels for 6% -> 6%
where the time goes in v4:
time: 192 us; the launch traced here: 190 us
  blocking collectives  59.6 us (31%)
  waiting for transfers between devices  55.7 us (29%)
  Pallas kernels  17.6 us (9%)
  starting transfers between devices  14.9 us (8%)
  between operations  13.5 us (7%)
  matrix products  12.4 us (6%)
  other arithmetic  9.73 us (5%)
  local copies, waits for them, and re-layouts  6.85 us (4%)
    all_to_all x1, blocking collectives, body(): lax.all_to_all(screened, 'ao', split_axis=0, concat_axis=1, tiled=True)[0]  39.6 us
    all_to_all x1, waiting for transfers between devices, body(): lax.all_to_all(products, ALL, split_axis=0, concat_axis=0, tiled=True, ax...  30.8 us
    all_to_all x1, blocking collectives, body(): lax.all_to_all(parcels, ALL, split_axis=0, concat_axis=0, tiled=True, axi...  20 us
    all_gather x1, waiting for transfers between devices, body(): lax.all_gather(jnp.stack([occ_rows, virt_rows]), 'ao', axis=1, tiled=True)  19.5 us
    dot_general x1, matrix products, body(): lax.dot_general(tensor_slab, virt, (((2,), (1,)), ((), ())), preferred_el...  12.4 us
    pallas_call x2, Pallas kernels, occ_product(): pl.pallas_call(kernel, grid=(width // columns,), out_shape=jax.ShapeDtype...  11 us
    all_to_all x1, starting transfers between devices, body(): lax.all_to_all(products, ALL, split_axis=0, concat_axis=0, tiled=True, ax...  9.14 us
    pallas_call x1, Pallas kernels, final_product(): pl.pallas_call(kernel, grid=(width // columns,), out_shape=jax.ShapeDtype...  6.67 us
  transfers between devices with their start and end apart: 6, of which 4 were waited for; matrix products, arithmetic and copies ran while one was open for 11% of the time, Pallas kernels for 6%

profile of v4, /device:TPU:0, one launch (start us, length us, event | category | flops | bytes accessed | tf_op | source)
XLA Modules:
  0.0 190.3 jit_solution(13390945002937215224)
XLA Ops:
  6.5 0.0 all-gather.2.cloned.1.call-start
  6.5 0.7 convert_element_type.27
  7.2 0.1 broadcast_in_dim.9
  7.3 0.1 mul.30
  7.4 0.1 broadcast_in_dim.10
  7.5 0.1 mul.33
  7.5 1.0 dynamic-slice_multiply_fusion
  8.5 0.7 pad_maximum_fusion
  9.3 0.0 all-gather.2.cloned.1.call-update
  9.3 0.7 convert_bitcast_fusion.1
  10.0 0.1 broadcast_in_dim.11
  10.1 0.1 convert_element_type.30
  10.1 0.0 copy-start.3
  10.1 1.9 broadcast_multiply_fusion
  12.0 39.6 %all_to_all.39 = bf16[16,64,1024]{2,1,0:T(8,128)(2,1)} all-to-all(bf16[16,64,1024]{2,1,0:T(8,128)(2,1)S(1)} %broadcast_multiply_fusion), channel_id=1, replica_groups=mesh['ao'=16,'aux'=8] {'ao'}, dimensions={0} | all-to-all | bytes 4194304 | tf_op jit(solution)/shard_map/all_to_all | solution.py:122
  51.7 0.0 collective-permute-start
  51.7 0.0 copy-done.3
  51.7 0.1 fusion.5
  51.8 1.5 copy.23
  53.3 5.4 %all-to-all-start.1 = ((bf16[16,8,8,1024]{3,2,0,1:T(8,128)(2,1)}), bf16[16,8,8,1024]{3,2,0,1:T(8,128)(2,1)S(1)}, u32[]{:S(2)}, u32[]{:S(2)}) async-start(bf16[16,8,8,1024]{3,2,0,1:T(8,128)(2,1)} %copy.23), calls=%async_computation.1 | async-start | bytes 4194304 | tf_op jit(solution)/shard_map/all_to_all | solution.py:125
  58.7 19.5 %all-gather.2.cloned.1.call-done.occ_ref = bf16[2,1024,1024]{2,1,0:T(8,128)(2,1)} async-done(((bf16[2,64,1024]{2,1,0:T(8,128)(2,1)}), bf16[2,1024,1024]{2,1,0:T(8,128)(2,1)}) %all-gather.2.cloned.1.call-update) | async-done | bytes 4194320 | tf_op jit(solution)/shard_map/all_gather | solution.py:118
  78.3 5.5 %shard_map.55.refs_0_ = bf16[64,2,16,1024]{3,2,1,0:T(8,128)(2,1)} custom-call(bf16[2,1024,1024]{2,1,0:T(8,128)(2,1)} %all-gather.2.cloned.1.call-done.occ_ref, bf16[1024,1024]{1,0:T(8,128)(2,1)} %bitcast.3.matrix_ref), custom_call_target="tpu_custom_call" | custom-call | flops 2147483648 | bytes 6291456 | tf_op jit(solution)/shard_map/pallas_call | solution.py:49
  83.7 0.0 collective-permute-done.matrix_ref
  83.7 5.5 %shard_map.56.refs_0_ = bf16[64,2,16,1024]{3,2,1,0:T(8,128)(2,1)} custom-call(bf16[2,1024,1024]{2,1,0:T(8,128)(2,1)} %all-gather.2.cloned.1.call-done.occ_ref, bf16[1024,1024]{1,0:T(8,128)(2,1)} %collective-permute-done.matrix_ref, bf16[64,2,16,1024]{3,2,1,0:T(8,128)(2,1)} %shard_map.55.refs_0_), custom_call_target="tpu_custom_call", output_to_operand_aliasing={{}: (2, {})} | custom-call | flops 2147483648 | bytes 6291456 | tf_op jit(solution)/shard_map/pallas_call | solution.py:49
  89.2 0.0 all-to-all-done.1
  89.2 1.3 copy-done
  90.6 9.1 %all-to-all-start.2 = ((bf16[64,2,16,1024]{3,2,1,0:T(8,128)(2,1)}), bf16[64,2,16,1024]{3,2,1,0:T(8,128)(2,1)}, u32[]{:S(2)}, u32[]{:S(2)}) async-start(bf16[64,2,16,1024]{3,2,1,0:T(8,128)(2,1)} %shard_map.57), calls=%async_computation.2 | async-start | bytes 8388608 | tf_op jit(solution)/shard_map/all_to_all | solution.py:133
  99.7 0.0 copy-done.1
  99.7 0.3 collective-permute-start.1
  100.0 0.0 copy-start.2
  100.0 4.3 %collective-permute-done.1 = bf16[128,8,1024]{2,1,0:T(8,128)(2,1)} collective-permute-done((bf16[128,8,1024]{2,1,0:T(8,128)(2,1)S(1)}, bf16[128,8,1024]{2,1,0:T(8,128)(2,1)}, u32[]{:S(2)}, u32[]{:S(2)}) %collective-permute-start.1) | collective-permute-done | bytes 2097184 | tf_op jit(solution)/shard_map/ppermute | solution.py:128
  104.3 4.5 %maximum_select_fusion = bf16[128,16,1024]{2,1,0:T(8,128)(2,1)S(1)} fusion(bf16[128,8,1024]{2,1,0:T(8,128)(2,1)} %collective-permute-done.1, bf16[128,8,1024]{2,1,0:T(8,128)(2,1)S(1)} %bitcast.26, pred[]{:T(512)S(6)} %eq.6), kind=kLoop, calls=%fused_computation | loop fusion | flops 18874368 | bytes 8388609 | tf_op jit(solution)/shard_map/jit(_where)/select_n | solution.py:136
  108.8 0.0 copy-done.2
  108.8 12.4 %convert_bitcast_fusion.other_ref = bf16[16,1024,128]{2,1,0:T(8,128)(2,1)} fusion(bf16[128,16,1024]{2,1,0:T(8,128)(2,1)S(1)} %maximum_select_fusion, bf16[2,1024,1024]{2,1,0:T(8,128)(2,1)S(1)} %copy-done.2), kind=kOutput, calls=%fused_computation.3 | convolution fusion | flops 4297064448 | bytes 10485760 | tf_op jit(solution)/shard_map/dot_general | solution.py:139
  121.2 30.8 %all-to-all-done.2.got_ref = bf16[64,2,16,1024]{3,2,1,0:T(8,128)(2,1)} async-done(((bf16[64,2,16,1024]{3,2,1,0:T(8,128)(2,1)}), bf16[64,2,16,1024]{3,2,1,0:T(8,128)(2,1)}, u32[]{:S(2)}, u32[]{:S(2)}) %all-to-all-start.2) | async-done | bytes 4194336 | tf_op jit(solution)/shard_map/all_to_all | solution.py:133
  152.0 6.7 %shard_map.58 = f32[128,128]{1,0:T(8,128)} custom-call(bf16[64,2,16,1024]{3,2,1,0:T(8,128)(2,1)} %all-to-all-done.2.got_ref, bf16[16,1024,128]{2,1,0:T(8,128)(2,1)} %convert_bitcast_fusion.other_ref), custom_call_target="tpu_custom_call" | custom-call | flops 536870912 | bytes 8388608 | tf_op jit(solution)/shard_map/pallas_call | solution.py:88
  158.7 1.4 reshape.73
  160.1 0.6 copy.26
  160.7 0.5 all_to_all.34
  161.3 20.0 %all_to_all.40 = f32[64,1,256]{2,1,0:T(1,128)S(1)} all-to-all(f32[64,1,256]{2,1,0:T(1,128)S(1)} %all_to_all.34), channel_id=1, replica_groups={{0,2,4,6,8,10,12,14,16,18,20,22,24,26,28,30,32,34,36,38,40,42,44,46,48,..., dimensions={0} | all-to-all | bytes 131072 | tf_op jit(solution)/shard_map/all_to_all | solution.py:147
  181.2 0.1 reduce_sum.9
  181.3 0.1 squeeze.16
  181.4 0.1 collective-permute-start.2
  181.5 0.1 slice.51
  181.6 1.1 collective-permute-done.2
  182.7 0.1 copy.28
  182.7 0.1 copy.29
  182.8 0.7 copy.31
  (6 shorter events, 0.0 us)
Async XLA Ops:
  6.5 71.7 %all-gather.2.cloned.1.call-start = ((), (), s32[]{:S(2)}) async-start(), calls=%async_computation.4 | async-start | bytes 4456448 | tf_op jit(solution)/shard_map/all_gather | solution.py:118
  10.1 41.5 %copy-start.3 = (bf16[16,64,1024]{2,1,0:T(8,128)(2,1)S(1)}, bf16[16,64,1024]{2,1,0:T(8,128)(2,1)}, u32[]{:S(2)}) copy-start(bf16[16,64,1024]{2,1,0:T(8,128)(2,1)} %param.5) | copy-start | bytes 6291460
  51.7 32.1 %collective-permute-start = (bf16[1024,1024]{1,0:T(8,128)(2,1)}, bf16[1024,1024]{1,0:T(8,128)(2,1)}, u32[]{:S(2)}, u32[]{:S(2)}) collective-permute-start(bf16[1024,1024]{1,0:T(8,128)(2,1)} %bitcast.3.matrix_ref), channel_id=1, source_target_pairs={{0,1},{1,0},{2,3},{3,2},{4,5},{5,4},{6,7},{7,6},{8,9},{9,8},{10,11... | collective-permute-start | bytes 6291464 | tf_op jit(solution)/shard_map/ppermute | solution.py:123
  53.3 35.9 %all-to-all-start.1 = ((bf16[16,8,8,1024]{3,2,0,1:T(8,128)(2,1)}), bf16[16,8,8,1024]{3,2,0,1:T(8,128)(2,1)S(1)}, u32[]{:S(2)}, u32[]{:S(2)}) async-start(bf16[16,8,8,1024]{3,2,0,1:T(8,128)(2,1)} %copy.23), calls=%async_computation.1 | async-start | bytes 4194304 | tf_op jit(solution)/shard_map/all_to_all | solution.py:125
  89.2 1.3 copy-start
  90.6 9.2 %copy-start.1 = (bf16[16,8,8,1024]{3,2,0,1:T(8,128)(2,1)S(1)}, bf16[16,8,8,1024]{3,2,0,1:T(8,128)(2,1)}, u32[]{:S(2)}) copy-start(bf16[16,8,8,1024]{3,2,0,1:T(8,128)(2,1)} %copy-done) | copy-start | bytes 6291460
  90.6 61.4 %all-to-all-start.2 = ((bf16[64,2,16,1024]{3,2,1,0:T(8,128)(2,1)}), bf16[64,2,16,1024]{3,2,1,0:T(8,128)(2,1)}, u32[]{:S(2)}, u32[]{:S(2)}) async-start(bf16[64,2,16,1024]{3,2,1,0:T(8,128)(2,1)} %shard_map.57), calls=%async_computation.2 | async-start | bytes 8388608 | tf_op jit(solution)/shard_map/all_to_all | solution.py:133
  99.7 4.6 %collective-permute-start.1 = (bf16[128,8,1024]{2,1,0:T(8,128)(2,1)S(1)}, bf16[128,8,1024]{2,1,0:T(8,128)(2,1)}, u32[]{:S(2)}, u32[]{:S(2)}) collective-permute-start(bf16[128,8,1024]{2,1,0:T(8,128)(2,1)S(1)} %bitcast.25), channel_id=1, source_target_pairs={{0,1},{1,0},{2,3},{3,2},{4,5},{5,4},{6,7},{7,6},{8,9},{9,8},{10,11... | collective-permute-start | bytes 6291464 | tf_op jit(solution)/shard_map/ppermute | solution.py:128
  100.0 8.8 %copy-start.2 = (bf16[2,1024,1024]{2,1,0:T(8,128)(2,1)S(1)}, bf16[2,1024,1024]{2,1,0:T(8,128)(2,1)}, u32[]{:S(2)}) copy-start(bf16[2,1024,1024]{2,1,0:T(8,128)(2,1)} %all-gather.2.cloned.1.call-done.occ_ref) | copy-start | bytes 12582916
  181.4 1.2 collective-permute-start.2
Sparse Core Ops, SparseCore 0:
  9.5 68.7 all-gather.1

commit v5 on v4

--- a/solution.py
+++ b/solution.py
@@ -36,32 +36,27 @@
     )(value, *others)
 
 
-def occ_product(occ, matrix, into, index, *others):
-    depth, width = matrix.shape
-    first = isinstance(into, tuple)
-    shape = into if first else into.shape
-    columns = width // 2
+def occ_product(dens, matrices, slab):
+    depth, width = matrices[0].shape
+    count, columns = len(matrices), width // 4
 
-    def kernel(occ_ref, matrix_ref, *refs):
-        product = jnp.dot(occ_ref[0], matrix_ref[...], preferred_element_type=jnp.float32)
-        refs[-1][...] = product.astype(jnp.bfloat16).reshape(refs[-1].shape)
+    def kernel(occ_ref, *refs):
+        for n in range(count):
+            product = jnp.dot(occ_ref[0], refs[n][...], preferred_element_type=jnp.float32)
+            refs[-1][:, n] = product.astype(jnp.bfloat16).reshape(depth // slab, slab, columns)
 
     return pl.pallas_call(
         kernel,
         grid=(width // columns,),
-        out_shape=jax.ShapeDtypeStruct(shape, jnp.bfloat16),
-        in_specs=[
-            pl.BlockSpec((1, depth, depth), lambda j: (0, 0, 0)),
-            pl.BlockSpec((depth, columns), lambda j: (0, j)),
-        ]
-        + [pl.BlockSpec(memory_space=pl.ANY)] * (len(others) + (not first)),
-        out_specs=pl.BlockSpec((shape[0], 1, shape[2], columns), lambda j: (0, index, 0, j)),
-        input_output_aliases={} if first else {2: 0},
+        out_shape=jax.ShapeDtypeStruct((depth // slab, count, slab, width), jnp.bfloat16),
+        in_specs=[pl.BlockSpec((1, depth, depth), lambda j: (0, 0, 0))]
+        + [pl.BlockSpec((depth, columns), lambda j: (0, j))] * count,
+        out_specs=pl.BlockSpec((depth // slab, count, slab, columns), lambda j: (0, 0, 0, j)),
         compiler_params=pltpu.CompilerParams(vmem_limit_bytes=56 * MIB),
         cost_estimate=pl.CostEstimate(
-            flops=2 * depth * depth * width, bytes_accessed=6 * depth * width, transcendentals=0
+            flops=2 * count * depth * depth * width, bytes_accessed=10 * depth * width, transcendentals=0
         ),
-    )(occ, matrix, *([] if first else [into]), *others)
+    )(dens, *matrices)
 
 
 def final_product(got, other):
@@ -70,14 +65,16 @@
     columns = width // 4
 
     def kernel(got_ref, other_ref, out_ref, wide):
-        total = jnp.zeros(out_ref.shape, jnp.float32)
         for part in range(columns // LANES):
             lanes = pl.ds(part * LANES, LANES)
             wide[part] = got_ref[..., lanes].reshape(wide.shape[1:]).astype(jnp.float32)
-        for row in range(slab):
-            left = [wide[part, pl.ds(row, sources * pair, stride=slab), :] for part in range(columns // LANES)]
-            left = jnp.concatenate(left, 1).astype(jnp.bfloat16)
-            total += jnp.dot(left, other_ref[row], preferred_element_type=jnp.float32)
+        left = [
+            wide[part, pl.ds(row, sources * pair, stride=slab), :].astype(jnp.bfloat16)
+            for row in range(slab)
+            for part in range(columns // LANES)
+        ]
+        right = other_ref[...].reshape(slab * columns, count)
+        total = jnp.dot(jnp.concatenate(left, 1), right, preferred_element_type=jnp.float32)
 
         @pl.when(pl.program_id(0) == 0)
         def _():
@@ -127,8 +124,7 @@
     ).reshape(groups * per_group, -1, width)
     slabs_other = lax.ppermute(slabs, "aux", OTHER_CORE)
 
-    products = occ_product(dens, own, (chips, CORES, slab, width), 0)
-    products = occ_product(dens, twin, products, 1)
+    products = occ_product(dens, (own, twin), slab)
     products = hold(products, slabs)
     got = lax.all_to_all(
         products, ALL, split_axis=0, concat_axis=0, tiled=True, axis_index_groups=SAME_CORE
@@ -143,12 +139,10 @@
 
     part = final_product(got, other)
     part = part.reshape(SIDE * SIDE, SIDE, CORES, SIDE * SIDE, -1)
-    parcels = jnp.transpose(part, (3, 1, 2, 0, 4)).reshape(chips, -1)
-    summed = lax.all_to_all(
-        parcels, ALL, split_axis=0, concat_axis=0, tiled=True, axis_index_groups=SAME_CORE
-    ).sum(axis=0).reshape(CORES, per_group, -1)
-    mine, theirs = summed[0], lax.ppermute(summed[1], "aux", OTHER_CORE)
-    return jnp.where(core == 0, jnp.stack([mine, theirs]), jnp.stack([theirs, mine]))
+    part = jnp.where(core == 0, part, part[:, :, ::-1])
+    parcels = jnp.transpose(part, (3, 1, 2, 0, 4)).reshape(chips * CORES, -1)
+    parts = lax.all_to_all(parcels, ALL, split_axis=0, concat_axis=0, tiled=True)
+    return parts.reshape(chips, CORES, -1).sum(axis=0).reshape(CORES, per_group, -1)
 
 
 def solution(mesh):

time: 192 us -> 187 us (0.974)
  Pallas kernels: 17.6 us -> 15.1 us
    pallas_call x2 -> x1, Pallas kernels: 11 us -> 8.45 us  [occ_product(): pl.pallas_call(kernel, grid=(width // columns,), out_shape=jax.ShapeDtype...]
  transfers between devices with their start and end apart: 6 -> 5, of which waited for: 4 -> 3; matrix products, arithmetic and copies ran while one was open for 11% -> 11% of each run, Pallas kernels for 6% -> 5%
where the time goes in v5:
time: 187 us; the launch traced here: 186 us
  blocking collectives  59.1 us (32%)
  waiting for transfers between devices  54.6 us (29%)
  Pallas kernels  15.1 us (8%)
  starting transfers between devices  14.8 us (8%)
  between operations  13.5 us (7%)
  matrix products  12.4 us (7%)
  other arithmetic  9.83 us (5%)
  local copies, waits for them, and re-layouts  6.57 us (4%)
    all_to_all x1, blocking collectives, body(): lax.all_to_all(screened, 'ao', split_axis=0, concat_axis=1, tiled=True)[0]  39.6 us
    all_to_all x1, waiting for transfers between devices, body(): lax.all_to_all(products, ALL, split_axis=0, concat_axis=0, tiled=True, ax...  30.8 us
    all_gather x1, waiting for transfers between devices, body(): lax.all_gather(jnp.stack([occ_rows, virt_rows]), 'ao', axis=1, tiled=True)  19.6 us
    all_to_all x1, blocking collectives, body(): lax.all_to_all(parcels, ALL, split_axis=0, concat_axis=0, tiled=True)  19.5 us
    dot_general x1, matrix products, body(): lax.dot_general(tensor_slab, virt, (((2,), (1,)), ((), ())), preferred_el...  12.4 us
    all_to_all x1, starting transfers between devices, body(): lax.all_to_all(products, ALL, split_axis=0, concat_axis=0, tiled=True, ax...  9.14 us
    pallas_call x1, Pallas kernels, occ_product(): pl.pallas_call(kernel, grid=(width // columns,), out_shape=jax.ShapeDtype...  8.45 us
    pallas_call x1, Pallas kernels, final_product(): pl.pallas_call(kernel, grid=(width // columns,), out_shape=jax.ShapeDtype...  6.68 us
  transfers between devices with their start and end apart: 5, of which 3 were waited for; matrix products, arithmetic and copies ran while one was open for 11% of the time, Pallas kernels for 5%

profile of v5, /device:TPU:0, one launch (start us, length us, event | category | flops | bytes accessed | tf_op | source)
XLA Modules:
  0.0 186.0 jit_solution(15201700928003112558)
XLA Ops:
  6.5 0.0 all-gather.2.cloned.1.call-start
  6.5 0.7 convert_element_type.27
  7.2 0.1 broadcast_in_dim.9
  7.3 0.1 mul.30
  7.4 0.1 broadcast_in_dim.10
  7.5 0.1 mul.33
  7.5 1.0 dynamic-slice_multiply_fusion
  8.5 0.8 pad_maximum_fusion
  9.3 0.0 all-gather.2.cloned.1.call-update
  9.3 0.7 convert_bitcast_fusion.1
  10.0 0.1 broadcast_in_dim.11
  10.1 0.1 convert_element_type.30
  10.2 0.0 copy-start.2
  10.2 1.9 %broadcast_multiply_fusion = bf16[16,64,1024]{2,1,0:T(8,128)(2,1)S(1)} fusion(bf16[16,64,1024]{2,1,0:T(8,128)(2,1)} %param.5, bf16[1024]{0:T(1024)(128)(2,1)S(1)} %convert_element_type.30), kind=kLoop, calls=%fused_computation.7 | loop fusion | flops 1048576 | bytes 4196352 | tf_op jit(solution)/shard_map/mul | solution.py:118
  12.0 39.6 %all_to_all.38 = bf16[16,64,1024]{2,1,0:T(8,128)(2,1)} all-to-all(bf16[16,64,1024]{2,1,0:T(8,128)(2,1)S(1)} %broadcast_multiply_fusion), channel_id=1, replica_groups=mesh['ao'=16,'aux'=8] {'ao'}, dimensions={0} | all-to-all | bytes 4194304 | tf_op jit(solution)/shard_map/all_to_all | solution.py:119
  51.7 0.0 collective-permute-start
  51.7 0.0 copy-done.2
  51.7 0.1 fusion.5
  51.8 1.5 copy.15
  53.3 5.4 %all-to-all-start.1 = ((bf16[16,8,8,1024]{3,2,0,1:T(8,128)(2,1)}), bf16[16,8,8,1024]{3,2,0,1:T(8,128)(2,1)S(1)}, u32[]{:S(2)}, u32[]{:S(2)}) async-start(bf16[16,8,8,1024]{3,2,0,1:T(8,128)(2,1)} %copy.15), calls=%async_computation.1 | async-start | bytes 4194304 | tf_op jit(solution)/shard_map/all_to_all | solution.py:122
  58.7 0.0 collective-permute-done.refs_1_
  58.7 19.6 %all-gather.2.cloned.1.call-done.occ_ref = bf16[2,1024,1024]{2,1,0:T(8,128)(2,1)} async-done(((bf16[2,64,1024]{2,1,0:T(8,128)(2,1)}), bf16[2,1024,1024]{2,1,0:T(8,128)(2,1)}) %all-gather.2.cloned.1.call-update) | async-done | bytes 4194320 | tf_op jit(solution)/shard_map/all_gather | solution.py:115
  78.3 8.4 %shard_map.55.refs_0_ = bf16[64,2,16,1024]{3,2,1,0:T(8,128)(2,1)} custom-call(bf16[2,1024,1024]{2,1,0:T(8,128)(2,1)} %all-gather.2.cloned.1.call-done.occ_ref, bf16[1024,1024]{1,0:T(8,128)(2,1)} %bitcast.3.refs_0_, bf16[1024,1024]{1,0:T(8,128)(2,1)} %collective-permute-done.refs_1_), custom_call_target="tpu_custom_call" | custom-call | flops 4294967296 | bytes 10485760 | tf_op jit(solution)/shard_map/pallas_call | solution.py:48
  86.7 0.0 all-to-all-done.1
  86.7 0.0 copy-start
  86.7 1.3 copy-done
  88.0 0.0 copy-start.1
  88.1 9.1 %all-to-all-start.2 = ((bf16[64,2,16,1024]{3,2,1,0:T(8,128)(2,1)}), bf16[64,2,16,1024]{3,2,1,0:T(8,128)(2,1)}, u32[]{:S(2)}, u32[]{:S(2)}) async-start(bf16[64,2,16,1024]{3,2,1,0:T(8,128)(2,1)} %shard_map.56), calls=%async_computation.2 | async-start | bytes 8388608 | tf_op jit(solution)/shard_map/all_to_all | solution.py:129
  97.2 0.0 copy-done.1
  97.2 0.3 collective-permute-start.1
  97.5 0.0 copy-start.3
  97.5 4.3 %collective-permute-done.1 = bf16[128,8,1024]{2,1,0:T(8,128)(2,1)} collective-permute-done((bf16[128,8,1024]{2,1,0:T(8,128)(2,1)S(1)}, bf16[128,8,1024]{2,1,0:T(8,128)(2,1)}, u32[]{:S(2)}, u32[]{:S(2)}) %collective-permute-start.1) | collective-permute-done | bytes 2097184 | tf_op jit(solution)/shard_map/ppermute | solution.py:125
  101.8 4.5 %maximum_select_fusion = bf16[128,16,1024]{2,1,0:T(8,128)(2,1)S(1)} fusion(bf16[128,8,1024]{2,1,0:T(8,128)(2,1)} %collective-permute-done.1, bf16[128,8,1024]{2,1,0:T(8,128)(2,1)S(1)} %bitcast.28, pred[]{:T(512)S(6)} %eq.6), kind=kLoop, calls=%fused_computation | loop fusion | flops 18874368 | bytes 8388609 | tf_op jit(solution)/shard_map/jit(_where)/select_n | solution.py:132
  106.3 0.0 copy-done.3
  106.3 12.4 %convert_bitcast_fusion.other_ref = bf16[16,1024,128]{2,1,0:T(8,128)(2,1)} fusion(bf16[128,16,1024]{2,1,0:T(8,128)(2,1)S(1)} %maximum_select_fusion, bf16[2,1024,1024]{2,1,0:T(8,128)(2,1)S(1)} %copy-done.3), kind=kOutput, calls=%fused_computation.3 | convolution fusion | flops 4297064448 | bytes 10485760 | tf_op jit(solution)/shard_map/dot_general | solution.py:135
  118.7 30.8 %all-to-all-done.2.got_ref = bf16[64,2,16,1024]{3,2,1,0:T(8,128)(2,1)} async-done(((bf16[64,2,16,1024]{3,2,1,0:T(8,128)(2,1)}), bf16[64,2,16,1024]{3,2,1,0:T(8,128)(2,1)}, u32[]{:S(2)}, u32[]{:S(2)}) %all-to-all-start.2) | async-done | bytes 4194336 | tf_op jit(solution)/shard_map/all_to_all | solution.py:129
  149.5 6.7 %shard_map.57 = f32[128,128]{1,0:T(8,128)} custom-call(bf16[64,2,16,1024]{3,2,1,0:T(8,128)(2,1)} %all-to-all-done.2.got_ref, bf16[16,1024,128]{2,1,0:T(8,128)(2,1)} %convert_bitcast_fusion.other_ref), custom_call_target="tpu_custom_call" | custom-call | flops 536870912 | bytes 8388608 | tf_op jit(solution)/shard_map/pallas_call | solution.py:85
  156.2 1.4 reshape.60
  157.6 0.1 fusion.4
  157.7 0.6 copy.18
  158.3 0.5 all_to_all.32
  158.8 19.5 %all_to_all.39 = f32[128,1,128]{2,1,0:T(1,128)S(1)} all-to-all(f32[128,1,128]{2,1,0:T(1,128)S(1)} %bitcast.29), channel_id=1, replica_groups=mesh['ao'=16,'aux'=8] {'ao','aux'}, dimensions={0} | all-to-all | bytes 131072 | tf_op jit(solution)/shard_map/all_to_all | solution.py:144
  178.3 0.1 reduce_sum.9
  178.4 0.1 reshape.62
  178.5 0.7 copy.20
  (2 shorter events, 0.0 us)
Async XLA Ops:
  6.5 71.7 %all-gather.2.cloned.1.call-start = ((), (), s32[]{:S(2)}) async-start(), calls=%async_computation.4 | async-start | bytes 4456448 | tf_op jit(solution)/shard_map/all_gather | solution.py:115
  10.2 41.5 %copy-start.2 = (bf16[16,64,1024]{2,1,0:T(8,128)(2,1)S(1)}, bf16[16,64,1024]{2,1,0:T(8,128)(2,1)}, u32[]{:S(2)}) copy-start(bf16[16,64,1024]{2,1,0:T(8,128)(2,1)} %param.5) | copy-start | bytes 6291460
  51.7 7.1 %collective-permute-start = (bf16[1024,1024]{1,0:T(8,128)(2,1)}, bf16[1024,1024]{1,0:T(8,128)(2,1)}, u32[]{:S(2)}, u32[]{:S(2)}) collective-permute-start(bf16[1024,1024]{1,0:T(8,128)(2,1)} %bitcast.3.refs_0_), channel_id=1, source_target_pairs={{0,1},{1,0},{2,3},{3,2},{4,5},{5,4},{6,7},{7,6},{8,9},{9,8},{10,11... | collective-permute-start | bytes 6291464 | tf_op jit(solution)/shard_map/ppermute | solution.py:120
  53.3 33.4 %all-to-all-start.1 = ((bf16[16,8,8,1024]{3,2,0,1:T(8,128)(2,1)}), bf16[16,8,8,1024]{3,2,0,1:T(8,128)(2,1)S(1)}, u32[]{:S(2)}, u32[]{:S(2)}) async-start(bf16[16,8,8,1024]{3,2,0,1:T(8,128)(2,1)} %copy.15), calls=%async_computation.1 | async-start | bytes 4194304 | tf_op jit(solution)/shard_map/all_to_all | solution.py:122
  86.7 1.3 copy-start
  88.0 9.2 %copy-start.1 = (bf16[16,8,8,1024]{3,2,0,1:T(8,128)(2,1)S(1)}, bf16[16,8,8,1024]{3,2,0,1:T(8,128)(2,1)}, u32[]{:S(2)}) copy-start(bf16[16,8,8,1024]{3,2,0,1:T(8,128)(2,1)} %copy-done) | copy-start | bytes 6291460
  88.1 61.4 %all-to-all-start.2 = ((bf16[64,2,16,1024]{3,2,1,0:T(8,128)(2,1)}), bf16[64,2,16,1024]{3,2,1,0:T(8,128)(2,1)}, u32[]{:S(2)}, u32[]{:S(2)}) async-start(bf16[64,2,16,1024]{3,2,1,0:T(8,128)(2,1)} %shard_map.56), calls=%async_computation.2 | async-start | bytes 8388608 | tf_op jit(solution)/shard_map/all_to_all | solution.py:129
  97.2 4.6 %collective-permute-start.1 = (bf16[128,8,1024]{2,1,0:T(8,128)(2,1)S(1)}, bf16[128,8,1024]{2,1,0:T(8,128)(2,1)}, u32[]{:S(2)}, u32[]{:S(2)}) collective-permute-start(bf16[128,8,1024]{2,1,0:T(8,128)(2,1)S(1)} %bitcast.27), channel_id=1, source_target_pairs={{0,1},{1,0},{2,3},{3,2},{4,5},{5,4},{6,7},{7,6},{8,9},{9,8},{10,11... | collective-permute-start | bytes 6291464 | tf_op jit(solution)/shard_map/ppermute | solution.py:125
  97.5 8.8 %copy-start.3 = (bf16[2,1024,1024]{2,1,0:T(8,128)(2,1)S(1)}, bf16[2,1024,1024]{2,1,0:T(8,128)(2,1)}, u32[]{:S(2)}) copy-start(bf16[2,1024,1024]{2,1,0:T(8,128)(2,1)} %all-gather.2.cloned.1.call-done.occ_ref) | copy-start | bytes 12582916
Sparse Core Ops, SparseCore 0:
  9.5 68.7 all-gather.1

commit v6 on v5

--- a/solution.py
+++ b/solution.py
@@ -20,20 +20,6 @@
 
 def expand(mask_row, width):
     return jnp.repeat(mask_row, width, axis=-1).astype(jnp.bfloat16)
-
-
-def hold(value, *others):
-    def kernel(*refs):
-        pass
-
-    whole = pl.BlockSpec(memory_space=pl.ANY)
-    return pl.pallas_call(
-        kernel,
-        out_shape=jax.ShapeDtypeStruct(value.shape, value.dtype),
-        in_specs=[whole] * (1 + len(others)),
-        out_specs=whole,
-        input_output_aliases={0: 0},
-    )(value, *others)
 
 
 def occ_product(dens, matrices, slab):
@@ -125,7 +111,6 @@
     slabs_other = lax.ppermute(slabs, "aux", OTHER_CORE)
 
     products = occ_product(dens, (own, twin), slab)
-    products = hold(products, slabs)
     got = lax.all_to_all(
         products, ALL, split_axis=0, concat_axis=0, tiled=True, axis_index_groups=SAME_CORE
     )

time: 187 us -> 185 us (0.989)
  waiting for transfers between devices: 54.6 us -> 60.7 us
  other arithmetic: 9.83 us -> 5.12 us
  matrix products: 12.4 us -> 8.61 us
    all_to_all x1, waiting for transfers between devices: 30.8 us -> 36.8 us  [body(): lax.all_to_all(products, ALL, split_axis=0, concat_axis=0, tiled=True, ax...]
    select_n x1 -> x0, other arithmetic: 4.52 us -> none  [body(): jnp.where(core == 0, jnp.concatenate([slabs, slabs_other], 1), jnp.concat...]
    dot_general x1, matrix products: 12.4 us -> 8.61 us  [body(): lax.dot_general(tensor_slab, virt, (((2,), (1,)), ((), ())), preferred_el...]
    reshape x0 -> x1, local copies, waits for them, and re-layouts: none -> 2.49 us  [body(): slabs = lax.all_to_all(screened.reshape(per_group, groups, -1, width), 'a...]
  transfers between devices with their start and end apart: 5 -> 5, of which waited for: 3 -> 3; matrix products, arithmetic and copies ran while one was open for 11% -> 8% of each run, Pallas kernels for 5% -> 5%
where the time goes in v6:
time: 185 us
  waiting for transfers between devices  60.7 us (33%)
  blocking collectives  59.3 us (32%)
  Pallas kernels  15.2 us (8%)
  starting transfers between devices  14.4 us (8%)
  between operations  13.5 us (7%)
  matrix products  8.61 us (5%)
  local copies, waits for them, and re-layouts  7.76 us (4%)
  other arithmetic  5.12 us (3%)
    all_to_all x1, blocking collectives, body(): lax.all_to_all(screened, 'ao', split_axis=0, concat_axis=1, tiled=True)[0]  39.8 us
    all_to_all x1, waiting for transfers between devices, body(): lax.all_to_all(products, ALL, split_axis=0, concat_axis=0, tiled=True, ax...  36.8 us
    all_gather x1, waiting for transfers between devices, body(): lax.all_gather(jnp.stack([occ_rows, virt_rows]), 'ao', axis=1, tiled=True)  19.5 us
    all_to_all x1, blocking collectives, body(): lax.all_to_all(parcels, ALL, split_axis=0, concat_axis=0, tiled=True)  19.5 us
    all_to_all x1, starting transfers between devices, body(): lax.all_to_all(products, ALL, split_axis=0, concat_axis=0, tiled=True, ax...  9.01 us
    dot_general x1, matrix products, body(): lax.dot_general(tensor_slab, virt, (((2,), (1,)), ((), ())), preferred_el...  8.61 us
    pallas_call x1, Pallas kernels, occ_product(): pl.pallas_call(kernel, grid=(width // columns,), out_shape=jax.ShapeDtype...  8.51 us
    pallas_call x1, Pallas kernels, final_product(): pl.pallas_call(kernel, grid=(width // columns,), out_shape=jax.ShapeDtype...  6.66 us
  transfers between devices with their start and end apart: 5, of which 3 were waited for; matrix products, arithmetic and copies ran while one was open for 8% of the time, Pallas kernels for 5%

profile of v6, /device:TPU:0, one launch (start us, length us, event | category | flops | bytes accessed | tf_op | source)
XLA Modules:
  0.0 184.5 jit_solution(2074304648847701109)
XLA Ops:
  6.5 0.0 all-gather.2.cloned.1.call-start
  6.5 0.7 convert_element_type.27
  7.2 0.1 broadcast_in_dim.9
  7.3 0.1 mul.30
  7.4 0.1 broadcast_in_dim.10
  7.5 0.1 mul.33
  7.5 1.0 dynamic-slice_multiply_fusion
  8.5 0.7 pad_maximum_fusion
  9.3 0.0 all-gather.2.cloned.1.call-update
  9.3 0.7 convert_bitcast_fusion.1
  10.0 0.1 broadcast_in_dim.11
  10.0 0.1 convert_element_type.30
  10.1 1.7 broadcast_multiply_fusion
  11.8 0.0 copy-start
  11.9 39.8 %all_to_all.38 = bf16[16,64,1024]{2,1,0:T(8,128)(2,1)} all-to-all(bf16[16,64,1024]{2,1,0:T(8,128)(2,1)S(1)} %broadcast_multiply_fusion), channel_id=1, replica_groups=mesh['ao'=16,'aux'=8] {'ao'}, dimensions={0} | all-to-all | bytes 4194304 | tf_op jit(solution)/shard_map/all_to_all | solution.py:105
  51.6 0.0 collective-permute-start
  51.6 0.0 copy-done
  51.6 0.1 fusion.9
  51.8 1.5 copy.19
  53.3 5.4 %all-to-all-start.2 = ((bf16[16,8,8,1024]{3,2,0,1:T(8,128)(2,1)}), bf16[16,8,8,1024]{3,2,0,1:T(8,128)(2,1)S(1)}, u32[]{:S(2)}, u32[]{:S(2)}) async-start(bf16[16,8,8,1024]{3,2,0,1:T(8,128)(2,1)} %copy.19), calls=%async_computation.2 | async-start | bytes 4194304 | tf_op jit(solution)/shard_map/all_to_all | solution.py:108
  58.7 0.0 collective-permute-done.refs_1_
  58.7 19.5 %all-gather.2.cloned.1.call-done.occ_ref = bf16[2,1024,1024]{2,1,0:T(8,128)(2,1)} async-done(((bf16[2,64,1024]{2,1,0:T(8,128)(2,1)}), bf16[2,1024,1024]{2,1,0:T(8,128)(2,1)}) %all-gather.2.cloned.1.call-update) | async-done | bytes 4194320 | tf_op jit(solution)/shard_map/all_gather | solution.py:101
  78.2 8.5 %shard_map.55 = bf16[64,2,16,1024]{3,2,1,0:T(8,128)(2,1)} custom-call(bf16[2,1024,1024]{2,1,0:T(8,128)(2,1)} %all-gather.2.cloned.1.call-done.occ_ref, bf16[1024,1024]{1,0:T(8,128)(2,1)} %bitcast.3.refs_0_, bf16[1024,1024]{1,0:T(8,128)(2,1)} %collective-permute-done.refs_1_), custom_call_target="tpu_custom_call" | custom-call | flops 4294967296 | bytes 10485760 | tf_op jit(solution)/shard_map/pallas_call | solution.py:34
  86.7 0.0 all-to-all-done.2
  86.7 9.0 %all-to-all-start.1 = ((bf16[64,2,16,1024]{3,2,1,0:T(8,128)(2,1)}), bf16[64,2,16,1024]{3,2,1,0:T(8,128)(2,1)}, u32[]{:S(2)}, u32[]{:S(2)}) async-start(bf16[64,2,16,1024]{3,2,1,0:T(8,128)(2,1)} %shard_map.55), calls=%async_computation.1 | async-start | bytes 8388608 | tf_op jit(solution)/shard_map/all_to_all | solution.py:114
  95.8 2.5 %copy.21 = bf16[128,8,1024]{2,0,1:T(8,128)(2,1)} copy(bf16[128,8,1024]{2,1,0:T(8,128)(2,1)S(1)} %bitcast.26) | data formatting | bytes 4194304 | tf_op jit(solution)/shard_map/reshape | solution.py:110
  98.2 0.0 collective-permute-start.1
  98.2 4.4 %collective-permute-done.1 = bf16[128,8,1024]{2,0,1:T(8,128)(2,1)S(1)} collective-permute-done((bf16[128,8,1024]{2,0,1:T(8,128)(2,1)}, bf16[128,8,1024]{2,0,1:T(8,128)(2,1)S(1)}, u32[]{:S(2)}, u32[]{:S(2)}) %collective-permute-start.1) | collective-permute-done | bytes 2097184 | tf_op jit(solution)/shard_map/ppermute | solution.py:111
  102.6 8.6 %convert_bitcast_fusion.other_ref = bf16[16,1024,128]{2,1,0:T(8,128)(2,1)} fusion(bf16[128,8,1024]{2,0,1:T(8,128)(2,1)S(1)} %collective-permute-done.1, bf16[128,8,1024]{2,0,1:T(8,128)(2,1)} %copy.21, pred[]{:T(512)S(6)} %eq.6, bf16[2,1024,1024]{2,1,0:T(8,128)(2,1)} %all-gather.2.cloned.1.call-done.occ_ref), kind=kOutput, calls=%fused_computation.7 | convolution fusion | flops 4303355904 | bytes 10485761 | tf_op jit(solution)/shard_map/dot_general | solution.py:120
  111.2 36.8 %all-to-all-done.1.got_ref = bf16[64,2,16,1024]{3,2,1,0:T(8,128)(2,1)} async-done(((bf16[64,2,16,1024]{3,2,1,0:T(8,128)(2,1)}), bf16[64,2,16,1024]{3,2,1,0:T(8,128)(2,1)}, u32[]{:S(2)}, u32[]{:S(2)}) %all-to-all-start.1) | async-done | bytes 4194336 | tf_op jit(solution)/shard_map/all_to_all | solution.py:114
  148.0 6.7 %shard_map.56 = f32[128,128]{1,0:T(8,128)} custom-call(bf16[64,2,16,1024]{3,2,1,0:T(8,128)(2,1)} %all-to-all-done.1.got_ref, bf16[16,1024,128]{2,1,0:T(8,128)(2,1)} %convert_bitcast_fusion.other_ref), custom_call_target="tpu_custom_call" | custom-call | flops 536870912 | bytes 8388608 | tf_op jit(solution)/shard_map/pallas_call | solution.py:71
  154.7 1.4 reshape.60
  156.1 0.1 fusion.7
  156.2 0.6 copy.24
  156.8 0.5 all_to_all.32
  157.3 19.5 %all_to_all.39 = f32[128,1,128]{2,1,0:T(1,128)S(1)} all-to-all(f32[128,1,128]{2,1,0:T(1,128)S(1)} %bitcast.27), channel_id=1, replica_groups=mesh['ao'=16,'aux'=8] {'ao','aux'}, dimensions={0} | all-to-all | bytes 131072 | tf_op jit(solution)/shard_map/all_to_all | solution.py:129
  176.9 0.1 reduce_sum.9
  176.9 0.1 reshape.62
  177.0 0.7 copy.26
  (1 shorter events, 0.0 us)
Async XLA Ops:
  6.5 71.7 %all-gather.2.cloned.1.call-start = ((), (), s32[]{:S(2)}) async-start(), calls=%async_computation.4 | async-start | bytes 4456448 | tf_op jit(solution)/shard_map/all_gather | solution.py:101
  11.8 39.8 %copy-start = (bf16[16,64,1024]{2,1,0:T(8,128)(2,1)S(1)}, bf16[16,64,1024]{2,1,0:T(8,128)(2,1)}, u32[]{:S(2)}) copy-start(bf16[16,64,1024]{2,1,0:T(8,128)(2,1)} %param.5) | copy-start | bytes 6291460
  51.6 7.1 %collective-permute-start = (bf16[1024,1024]{1,0:T(8,128)(2,1)}, bf16[1024,1024]{1,0:T(8,128)(2,1)}, u32[]{:S(2)}, u32[]{:S(2)}) collective-permute-start(bf16[1024,1024]{1,0:T(8,128)(2,1)} %bitcast.3.refs_0_), channel_id=1, source_target_pairs={{0,1},{1,0},{2,3},{3,2},{4,5},{5,4},{6,7},{7,6},{8,9},{9,8},{10,11... | collective-permute-start | bytes 6291464 | tf_op jit(solution)/shard_map/ppermute | solution.py:106
  53.3 33.5 %all-to-all-start.2 = ((bf16[16,8,8,1024]{3,2,0,1:T(8,128)(2,1)}), bf16[16,8,8,1024]{3,2,0,1:T(8,128)(2,1)S(1)}, u32[]{:S(2)}, u32[]{:S(2)}) async-start(bf16[16,8,8,1024]{3,2,0,1:T(8,128)(2,1)} %copy.19), calls=%async_computation.2 | async-start | bytes 4194304 | tf_op jit(solution)/shard_map/all_to_all | solution.py:108
  86.7 61.3 %all-to-all-start.1 = ((bf16[64,2,16,1024]{3,2,1,0:T(8,128)(2,1)}), bf16[64,2,16,1024]{3,2,1,0:T(8,128)(2,1)}, u32[]{:S(2)}, u32[]{:S(2)}) async-start(bf16[64,2,16,1024]{3,2,1,0:T(8,128)(2,1)} %shard_map.55), calls=%async_computation.1 | async-start | bytes 8388608 | tf_op jit(solution)/shard_map/all_to_all | solution.py:114
  98.2 4.4 %collective-permute-start.1 = (bf16[128,8,1024]{2,0,1:T(8,128)(2,1)}, bf16[128,8,1024]{2,0,1:T(8,128)(2,1)S(1)}, u32[]{:S(2)}, u32[]{:S(2)}) collective-permute-start(bf16[128,8,1024]{2,0,1:T(8,128)(2,1)} %copy.21), channel_id=1, source_target_pairs={{0,1},{1,0},{2,3},{3,2},{4,5},{5,4},{6,7},{7,6},{8,9},{9,8},{10,11... | collective-permute-start | bytes 6291464 | tf_op jit(solution)/shard_map/ppermute | solution.py:111
Sparse Core Ops, SparseCore 0:
  9.5 68.6 all-gather.1

commit v7 on v6

--- a/solution.py
+++ b/solution.py
@@ -24,7 +24,7 @@
 
 def occ_product(dens, matrices, slab):
     depth, width = matrices[0].shape
-    count, columns = len(matrices), width // 4
+    count, columns = len(matrices), width // 2
 
     def kernel(occ_ref, *refs):
         for n in range(count):

time: 185 us -> 185 us (level)
  no operation moved by 1% of the time
where the time goes in v7:
time: 185 us
  waiting for transfers between devices  60.7 us (33%)
  blocking collectives  59.2 us (32%)
  Pallas kernels  15.3 us (8%)
  starting transfers between devices  14.4 us (8%)
  between operations  13.5 us (7%)
  matrix products  8.61 us (5%)
  local copies, waits for them, and re-layouts  7.76 us (4%)
  other arithmetic  5.12 us (3%)
    all_to_all x1, blocking collectives, body(): lax.all_to_all(screened, 'ao', split_axis=0, concat_axis=1, tiled=True)[0]  39.8 us
    all_to_all x1, waiting for transfers between devices, body(): lax.all_to_all(products, ALL, split_axis=0, concat_axis=0, tiled=True, ax...  36.8 us
    all_gather x1, waiting for transfers between devices, body(): lax.all_gather(jnp.stack([occ_rows, virt_rows]), 'ao', axis=1, tiled=True)  19.5 us
    all_to_all x1, blocking collectives, body(): lax.all_to_all(parcels, ALL, split_axis=0, concat_axis=0, tiled=True)  19.5 us
    all_to_all x1, starting transfers between devices, body(): lax.all_to_all(products, ALL, split_axis=0, concat_axis=0, tiled=True, ax...  9.02 us
    pallas_call x1, Pallas kernels, occ_product(): pl.pallas_call(kernel, grid=(width // columns,), out_shape=jax.ShapeDtype...  8.65 us
    dot_general x1, matrix products, body(): lax.dot_general(tensor_slab, virt, (((2,), (1,)), ((), ())), preferred_el...  8.61 us
    pallas_call x1, Pallas kernels, final_product(): pl.pallas_call(kernel, grid=(width // columns,), out_shape=jax.ShapeDtype...  6.66 us
  transfers between devices with their start and end apart: 5, of which 3 were waited for; matrix products, arithmetic and copies ran while one was open for 8% of the time, Pallas kernels for 5%

profile of v7, /device:TPU:0, one launch (start us, length us, event | category | flops | bytes accessed | tf_op | source)
XLA Modules:
  0.0 184.7 jit_solution(6309837572949294251)
XLA Ops:
  6.5 0.0 all-gather.2.cloned.1.call-start
  6.5 0.7 convert_element_type.27
  7.2 0.1 broadcast_in_dim.9
  7.3 0.1 mul.30
  7.4 0.1 broadcast_in_dim.10
  7.5 0.1 mul.33
  7.5 1.0 dynamic-slice_multiply_fusion
  8.5 0.7 pad_maximum_fusion
  9.3 0.0 all-gather.2.cloned.1.call-update
  9.3 0.7 convert_bitcast_fusion.1
  10.0 0.1 broadcast_in_dim.11
  10.0 0.1 convert_element_type.30
  10.1 1.7 broadcast_multiply_fusion
  11.8 0.0 copy-start
  11.9 39.8 %all_to_all.38 = bf16[16,64,1024]{2,1,0:T(8,128)(2,1)} all-to-all(bf16[16,64,1024]{2,1,0:T(8,128)(2,1)S(1)} %broadcast_multiply_fusion), channel_id=1, replica_groups=mesh['ao'=16,'aux'=8] {'ao'}, dimensions={0} | all-to-all | bytes 4194304 | tf_op jit(solution)/shard_map/all_to_all | solution.py:105
  51.6 0.0 collective-permute-start
  51.6 0.0 copy-done
  51.6 0.1 fusion.9
  51.8 1.5 copy.19
  53.3 5.4 %all-to-all-start.2 = ((bf16[16,8,8,1024]{3,2,0,1:T(8,128)(2,1)}), bf16[16,8,8,1024]{3,2,0,1:T(8,128)(2,1)S(1)}, u32[]{:S(2)}, u32[]{:S(2)}) async-start(bf16[16,8,8,1024]{3,2,0,1:T(8,128)(2,1)} %copy.19), calls=%async_computation.2 | async-start | bytes 4194304 | tf_op jit(solution)/shard_map/all_to_all | solution.py:108
  58.7 0.0 collective-permute-done.refs_1_
  58.7 19.5 %all-gather.2.cloned.1.call-done.occ_ref = bf16[2,1024,1024]{2,1,0:T(8,128)(2,1)} async-done(((bf16[2,64,1024]{2,1,0:T(8,128)(2,1)}), bf16[2,1024,1024]{2,1,0:T(8,128)(2,1)}) %all-gather.2.cloned.1.call-update) | async-done | bytes 4194320 | tf_op jit(solution)/shard_map/all_gather | solution.py:101
  78.2 8.7 %shard_map.55 = bf16[64,2,16,1024]{3,2,1,0:T(8,128)(2,1)} custom-call(bf16[2,1024,1024]{2,1,0:T(8,128)(2,1)} %all-gather.2.cloned.1.call-done.occ_ref, bf16[1024,1024]{1,0:T(8,128)(2,1)} %bitcast.3.refs_0_, bf16[1024,1024]{1,0:T(8,128)(2,1)} %collective-permute-done.refs_1_), custom_call_target="tpu_custom_call" | custom-call | flops 4294967296 | bytes 10485760 | tf_op jit(solution)/shard_map/pallas_call | solution.py:34
  86.9 0.0 all-to-all-done.2
  86.9 9.0 %all-to-all-start.1 = ((bf16[64,2,16,1024]{3,2,1,0:T(8,128)(2,1)}), bf16[64,2,16,1024]{3,2,1,0:T(8,128)(2,1)}, u32[]{:S(2)}, u32[]{:S(2)}) async-start(bf16[64,2,16,1024]{3,2,1,0:T(8,128)(2,1)} %shard_map.55), calls=%async_computation.1 | async-start | bytes 8388608 | tf_op jit(solution)/shard_map/all_to_all | solution.py:114
  95.9 2.5 %copy.21 = bf16[128,8,1024]{2,0,1:T(8,128)(2,1)} copy(bf16[128,8,1024]{2,1,0:T(8,128)(2,1)S(1)} %bitcast.26) | data formatting | bytes 4194304 | tf_op jit(solution)/shard_map/reshape | solution.py:110
  98.4 0.0 collective-permute-start.1
  98.4 4.4 %collective-permute-done.1 = bf16[128,8,1024]{2,0,1:T(8,128)(2,1)S(1)} collective-permute-done((bf16[128,8,1024]{2,0,1:T(8,128)(2,1)}, bf16[128,8,1024]{2,0,1:T(8,128)(2,1)S(1)}, u32[]{:S(2)}, u32[]{:S(2)}) %collective-permute-start.1) | collective-permute-done | bytes 2097184 | tf_op jit(solution)/shard_map/ppermute | solution.py:111
  102.8 8.6 %convert_bitcast_fusion.other_ref = bf16[16,1024,128]{2,1,0:T(8,128)(2,1)} fusion(bf16[128,8,1024]{2,0,1:T(8,128)(2,1)S(1)} %collective-permute-done.1, bf16[128,8,1024]{2,0,1:T(8,128)(2,1)} %copy.21, pred[]{:T(512)S(6)} %eq.6, bf16[2,1024,1024]{2,1,0:T(8,128)(2,1)} %all-gather.2.cloned.1.call-done.occ_ref), kind=kOutput, calls=%fused_computation.7 | convolution fusion | flops 4303355904 | bytes 10485761 | tf_op jit(solution)/shard_map/dot_general | solution.py:120
  111.4 36.8 %all-to-all-done.1.got_ref = bf16[64,2,16,1024]{3,2,1,0:T(8,128)(2,1)} async-done(((bf16[64,2,16,1024]{3,2,1,0:T(8,128)(2,1)}), bf16[64,2,16,1024]{3,2,1,0:T(8,128)(2,1)}, u32[]{:S(2)}, u32[]{:S(2)}) %all-to-all-start.1) | async-done | bytes 4194336 | tf_op jit(solution)/shard_map/all_to_all | solution.py:114
  148.2 6.7 %shard_map.56 = f32[128,128]{1,0:T(8,128)} custom-call(bf16[64,2,16,1024]{3,2,1,0:T(8,128)(2,1)} %all-to-all-done.1.got_ref, bf16[16,1024,128]{2,1,0:T(8,128)(2,1)} %convert_bitcast_fusion.other_ref), custom_call_target="tpu_custom_call" | custom-call | flops 536870912 | bytes 8388608 | tf_op jit(solution)/shard_map/pallas_call | solution.py:71
  154.9 1.4 reshape.60
  156.3 0.1 fusion.7
  156.4 0.6 copy.24
  157.0 0.5 all_to_all.32
  157.5 19.5 %all_to_all.39 = f32[128,1,128]{2,1,0:T(1,128)S(1)} all-to-all(f32[128,1,128]{2,1,0:T(1,128)S(1)} %bitcast.27), channel_id=1, replica_groups=mesh['ao'=16,'aux'=8] {'ao','aux'}, dimensions={0} | all-to-all | bytes 131072 | tf_op jit(solution)/shard_map/all_to_all | solution.py:129
  177.0 0.1 reduce_sum.9
  177.1 0.1 reshape.62
  177.2 0.7 copy.26
  (1 shorter events, 0.0 us)
Async XLA Ops:
  6.5 71.7 %all-gather.2.cloned.1.call-start = ((), (), s32[]{:S(2)}) async-start(), calls=%async_computation.4 | async-start | bytes 4456448 | tf_op jit(solution)/shard_map/all_gather | solution.py:101
  11.8 39.8 %copy-start = (bf16[16,64,1024]{2,1,0:T(8,128)(2,1)S(1)}, bf16[16,64,1024]{2,1,0:T(8,128)(2,1)}, u32[]{:S(2)}) copy-start(bf16[16,64,1024]{2,1,0:T(8,128)(2,1)} %param.5) | copy-start | bytes 6291460
  51.6 7.1 %collective-permute-start = (bf16[1024,1024]{1,0:T(8,128)(2,1)}, bf16[1024,1024]{1,0:T(8,128)(2,1)}, u32[]{:S(2)}, u32[]{:S(2)}) collective-permute-start(bf16[1024,1024]{1,0:T(8,128)(2,1)} %bitcast.3.refs_0_), channel_id=1, source_target_pairs={{0,1},{1,0},{2,3},{3,2},{4,5},{5,4},{6,7},{7,6},{8,9},{9,8},{10,11... | collective-permute-start | bytes 6291464 | tf_op jit(solution)/shard_map/ppermute | solution.py:106
  53.3 33.6 %all-to-all-start.2 = ((bf16[16,8,8,1024]{3,2,0,1:T(8,128)(2,1)}), bf16[16,8,8,1024]{3,2,0,1:T(8,128)(2,1)S(1)}, u32[]{:S(2)}, u32[]{:S(2)}) async-start(bf16[16,8,8,1024]{3,2,0,1:T(8,128)(2,1)} %copy.19), calls=%async_computation.2 | async-start | bytes 4194304 | tf_op jit(solution)/shard_map/all_to_all | solution.py:108
  86.9 61.3 %all-to-all-start.1 = ((bf16[64,2,16,1024]{3,2,1,0:T(8,128)(2,1)}), bf16[64,2,16,1024]{3,2,1,0:T(8,128)(2,1)}, u32[]{:S(2)}, u32[]{:S(2)}) async-start(bf16[64,2,16,1024]{3,2,1,0:T(8,128)(2,1)} %shard_map.55), calls=%async_computation.1 | async-start | bytes 8388608 | tf_op jit(solution)/shard_map/all_to_all | solution.py:114
  98.4 4.4 %collective-permute-start.1 = (bf16[128,8,1024]{2,0,1:T(8,128)(2,1)}, bf16[128,8,1024]{2,0,1:T(8,128)(2,1)S(1)}, u32[]{:S(2)}, u32[]{:S(2)}) collective-permute-start(bf16[128,8,1024]{2,0,1:T(8,128)(2,1)} %copy.21), channel_id=1, source_target_pairs={{0,1},{1,0},{2,3},{3,2},{4,5},{5,4},{6,7},{7,6},{8,9},{9,8},{10,11... | collective-permute-start | bytes 6291464 | tf_op jit(solution)/shard_map/ppermute | solution.py:111
Sparse Core Ops, SparseCore 0:
  9.5 68.6 all-gather.1
